TPU v7x, 32 devices: a whole 2x2x4 slice. The times are simulated.
32 devices in a mesh: groups: 1, dp: 16 (over z, y, x), tensor: 2 (over core).
Axes of the slice: x: 2, y: 2, z: 4, core: 2. Of those that a mesh axis runs over, the one named last changes fastest.
Arguments:
- normed: bfloat16 [8192, 5120], P(('groups', 'dp')), may hold values from -6 to 6
- cotangent: bfloat16 [8192, 1024], P(('groups', 'dp'), 'tensor'), may hold values from -6 to 6
- value_weight: bfloat16 [5120, 1024], P('dp', 'tensor'), may hold values from -0.078125 to 0.078125
- adapter_down_maps: bfloat16 [5120, 512], P('dp', 'groups'), may hold values from -0.078125 to 0.078125
- adapter_up_maps: bfloat16 [8, 64, 1024], P('groups', None, 'tensor'), may hold values from -0.19921875 to 0.19921875
- tenant_devices: int32 [8], P('groups'), may hold values from 1 to 9, as said below
- adapter_of: int32 [8], P('groups'), may hold values from 0 to 7, each once
- valid_tokens: int32 [8], P('groups'), may hold values from 1 to 4608, as said below
Outputs:
- values: bfloat16 [8192, 1024], P(('groups', 'dp'), 'tensor')
- normed_input_gradient: bfloat16 [8192, 5120], P(('groups', 'dp'), 'tensor')
- grad_a: float32 [16, 64, 5120], P(('groups', 'dp'), None, 'tensor')
- grad_b: float32 [16, 64, 1024], P(('groups', 'dp'), None, 'tensor')
Inputs may be any that keep to these rules, and one draw needn't show every extreme that they name: Slot s owns the next tenant_devices[s] shards along dp; the counts sum to 16, and the largest is exactly 9. valid_tokens[s] exceeds 512 times (tenant_devices[s] - 1) and is at most 512 times tenant_devices[s]; it equals that bound for the slot with the most devices. `adapter_of`: each adapter serves exactly one slot.
All inputs are finite; a program needn't handle non-finite values.
Results may differ from a plain program's by a relative error of at most 0.0032.
Values may be sent and summed in bfloat16 or wider, within the bound.
No kernel may reach another device: no remote copies, remote signals or barrier semaphores. Data moves between devices by JAX's collectives and lax.ppermute only.
A program may use at most 128 MiB of HBM per device.

v0:
```python
import jax
import jax.numpy as jnp
from jax import lax
from jax.sharding import PartitionSpec as P


def contract_last(left, right):
    return lax.dot_general(
        left, right, (((1,), (1,)), ((), ())), preferred_element_type=jnp.float32
    )


def contract_first(left, right):
    return lax.dot_general(
        left, right, (((0,), (0,)), ((), ())), preferred_element_type=jnp.float32
    )


def shards(
    normed,
    cotangent,
    value_weight,
    adapter_down_maps,
    adapter_up_maps,
    tenant_devices,
    adapter_of,
    valid_tokens,
):
    row_count = normed.shape[0]
    model_width = normed.shape[1]
    adapter_rank_rows = adapter_up_maps.shape[1]
    tenant_count = tenant_devices.shape[0]
    tensor_count = lax.axis_size("tensor")
    tensor_part = lax.axis_index("tensor")
    half_width = model_width // tensor_count
    position = lax.axis_index("dp")
    slot_ends = jnp.cumsum(tenant_devices)
    tenant_slot = jnp.sum((slot_ends <= position).astype(jnp.int32))
    picker = (jnp.arange(tenant_count, dtype=jnp.int32) == tenant_slot).astype(jnp.int32)
    first_device = jnp.sum(picker * (slot_ends - tenant_devices))
    adapter_index = jnp.sum(picker * adapter_of)
    valid_count = jnp.sum(picker * valid_tokens)
    offsets = (position - first_device) * row_count + jnp.arange(row_count, dtype=jnp.int32)
    keep_rows = offsets < valid_count
    up_matrix = lax.dynamic_index_in_dim(adapter_up_maps, adapter_index, 0, keepdims=False)
    weight_piece = lax.all_gather(value_weight, "dp", axis=0, tiled=True)
    adapter_slice = lax.all_gather(adapter_down_maps, "dp", axis=0, tiled=True)
    down_slice = lax.dynamic_slice_in_dim(
        adapter_slice, adapter_index * adapter_rank_rows, adapter_rank_rows, 1
    )
    base_acc = jnp.dot(normed, weight_piece, preferred_element_type=jnp.float32)
    low_acc = jnp.dot(normed, down_slice, preferred_element_type=jnp.float32)
    rank_projection = low_acc.astype(jnp.bfloat16)
    values = (
        base_acc + 2.0 * jnp.dot(rank_projection, up_matrix, preferred_element_type=jnp.float32)
    ).astype(jnp.bfloat16)
    masked = jnp.where(keep_rows[:, None], cotangent, jnp.zeros_like(cotangent))
    backward_rank_term = lax.psum(contract_last(masked, up_matrix), "tensor")
    scaled = (2.0 * backward_rank_term).astype(jnp.bfloat16)
    partial_terms = contract_last(masked, lax.all_gather(value_weight, "dp", axis=0, tiled=True))
    share_sum = lax.psum_scatter(partial_terms, "tensor", scatter_dimension=1, tiled=True)
    down_half = lax.dynamic_slice_in_dim(down_slice, tensor_part * half_width, half_width, 0)
    normed_input_gradient = (share_sum + contract_last(scaled, down_half)).astype(jnp.bfloat16)
    normed_half = lax.dynamic_slice_in_dim(normed, tensor_part * half_width, half_width, 1)
    term_a = contract_first(scaled, normed_half)
    term_b = 2.0 * contract_first(rank_projection, masked)
    slot_mark = picker.astype(jnp.float32)
    totals_a, totals_b = lax.psum(
        (slot_mark[:, None, None] * term_a[None], slot_mark[:, None, None] * term_b[None]), "dp"
    )
    grad_a = lax.dynamic_index_in_dim(totals_a, tenant_slot, 0, keepdims=True)
    grad_b = lax.dynamic_index_in_dim(totals_b, tenant_slot, 0, keepdims=True)
    return (values, normed_input_gradient, grad_a, grad_b)


def solution(mesh):
    return jax.shard_map(
        shards,
        mesh=mesh,
        in_specs=(
            P(("groups", "dp"), None),
            P(("groups", "dp"), "tensor"),
            P("dp", "tensor"),
            P("dp", "groups"),
            P("groups", None, "tensor"),
            P("groups"),
            P("groups"),
            P("groups"),
        ),
        out_specs=(
            P(("groups", "dp"), "tensor"),
            P(("groups", "dp"), "tensor"),
            P(("groups", "dp"), None, "tensor"),
            P(("groups", "dp"), None, "tensor"),
        ),
        check_vma=False,
    )
```

profile of v0, /device:TPU:0, one launch (start us, length us, event | category | flops | bytes accessed | tf_op | source)
XLA Modules:
  0.0 429.0 jit_solution(813615279192353364)
XLA Ops:
  8.1 0.9 reduce-window.9
  8.9 0.6 fusion.19
  9.6 1.9 fusion.21
  11.5 1.9 select_reduce_fusion.1
  15.4 1.9 select_reduce_fusion
  18.0 0.7 add_compare_fusion
  18.7 2.1 fusion.10
  20.8 0.5 all-gather.5.cloned.1.call-update
  21.4 0.5 all-gather.3.cloned.1.call-update
  22.6 0.7 convert_convert_fusion
  23.3 18.2 %all-reduce.4.cloned.1.call-done = f32[512,64]{0,1:T(8,128)} async-done(((f32[512,64]{0,1:T(8,128)}), f32[512,64]{0,1:T(8,128)}) %all-reduce.4.cloned.1.call-update) | async-done | bytes 131088 | tf_op jit(solution)/shard_map/psum | solution.py:58
  41.5 2.4 fusion
  43.9 3.0 broadcast_multiply_fusion
  46.9 64.2 %all-gather.5.cloned.1.call-done = bf16[5120,512]{1,0:T(8,128)(2,1)} async-done(((bf16[320,512]{1,0:T(8,128)(2,1)}), bf16[5120,512]{1,0:T(8,128)(2,1)}) %all-gather.5.cloned.1.call-update) | async-done | bytes 5242896 | tf_op jit(solution)/shard_map/all_gather | solution.py:47
  111.1 5.4 %fusion.6 = bf16[64,512]{1,0:T(8,128)(2,1)S(1)} fusion(bf16[512,5120]{1,0:T(8,128)(2,1)} %param.8, bf16[5120,512]{1,0:T(8,128)(2,1)} %all-gather.5.cloned.1.call-done, s32[]{:T(128)S(6)} %select_n.25), kind=kOutput, calls=%fused_computation.10 | convolution fusion | flops 335577088 | bytes 6619140 | tf_op jit(solution)/shard_map/dot_general | solution.py:52
  116.8 1.2 broadcast_multiply_fusion.1
  118.0 78.8 %all-gather.3.cloned.1.call-done = bf16[5120,512]{1,0:T(8,128)(2,1)} async-done(((bf16[320,512]{1,0:T(8,128)(2,1)}), bf16[5120,512]{1,0:T(8,128)(2,1)}) %all-gather.3.cloned.1.call-update) | async-done | bytes 5242896 | tf_op jit(solution)/shard_map/all_gather | solution.py:46
  196.8 8.1 %fusion.24 = f32[512,5120]{1,0:T(8,128)} fusion(bf16[5120,512]{1,0:T(8,128)(2,1)} %all-gather.3.cloned.1.call-done, bf16[512,512]{1,0:T(8,128)(2,1)S(1)} %copy-done.2, pred[512]{0:T(512)(128)(4,1)S(1)} %add_compare_fusion), kind=kOutput, calls=%fused_computation.38 | convolution fusion | flops 2684616704 | bytes 16253440 | tf_op jit(solution)/shard_map/dot_general | solution.py:8
  206.9 8.1 %fusion.25 = f32[512,512]{1,0:T(8,128)S(1)} fusion(bf16[512,5120]{1,0:T(8,128)(2,1)} %param.8, bf16[5120,512]{1,0:T(8,128)(2,1)} %all-gather.3.cloned.1.call-done), kind=kOutput, calls=%fused_computation.39 | convolution fusion | flops 2684354560 | bytes 11534336 | tf_op jit(solution)/shard_map/dot_general | solution.py:51
  215.0 1.1 fusion.5
  216.1 196.4 %all-reduce.6.cloned.1.call-done = (f32[8,64,2560]{2,1,0:T(8,128)}, f32[8,64,512]{2,1,0:T(8,128)}) async-done(((f32[8,64,2560]{2,1,0:T(8,128)}, f32[8,64,512]{2,1,0:T(8,128)}), (f32[8,64,2560]{2,1,0:T(8,128)}, f32[8,64,512]{2,1,0:T(8,128)})) %all-reduce.6.cloned.1.call-update) | async-done | bytes 6291472 | tf_op jit(solution)/shard_map/psum | solution.py:68
  412.5 1.6 constant_dynamic-slice_fusion
  414.1 2.0 constant_dynamic-slice_fusion.1
  416.1 5.4 %add_convert_fusion = bf16[512,2560]{1,0:T(8,128)(2,1)} fusion(f32[512,2560]{1,0:T(8,128)} %reduce-scatter.2.cloned.1.call-done, bf16[5120,512]{1,0:T(8,128)(2,1)} %all-gather.5.cloned.1.call-done, s32[]{:T(128)S(6)} %select_n.29, s32[]{:T(128)S(6)} %select_n.30, f32[512,64]{0,1:T(8,128)S(1)} %copy-done.1), kind=kOutput, calls=%fused_computation | convolution fusion | flops 170459136 | bytes 8650760 | tf_op jit(solution)/shard_map/dot_general | solution.py:8
  (16 shorter events, 0.6 us)
Async XLA Ops:
  8.0 10.7 %copy-start = (bf16[8,64,512]{2,1,0:T(8,128)(2,1)S(1)}, bf16[8,64,512]{2,1,0:T(8,128)(2,1)}, u32[]{:S(2)}) copy-start(bf16[8,64,512]{2,1,0:T(8,128)(2,1)} %param.12) | copy-start | bytes 1572868
  8.0 33.5 %all-reduce.4.cloned.1.call-start = ((), (), s32[]{:S(2)}) async-start(), calls=%async_computation.4 | async-start | bytes 262144 | tf_op jit(solution)/shard_map/psum | solution.py:58
  20.7 90.3 %all-gather.5.cloned.1.call-start = ((), (), s32[]{:S(2)}) async-start(), calls=%async_computation.2 | async-start | bytes 5570560 | tf_op jit(solution)/shard_map/all_gather | solution.py:47
  21.3 175.5 %all-gather.3.cloned.1.call-start = ((), (), s32[]{:S(2)}) async-start(), calls=%async_computation.1 | async-start | bytes 5570560 | tf_op jit(solution)/shard_map/all_gather | solution.py:46
  21.9 390.6 %all-reduce.6.cloned.1.call-start = ((), (), s32[]{:S(2)}) async-start(), calls=%async_computation.5 | async-start | bytes 12582912 | tf_op jit(solution)/shard_map/psum | solution.py:68
  43.9 72.6 %copy-start.2 = (bf16[512,512]{1,0:T(8,128)(2,1)S(1)}, bf16[512,512]{1,0:T(8,128)(2,1)}, u32[]{:S(2)}) copy-start(bf16[512,512]{1,0:T(8,128)(2,1)} %param.9) | copy-start | bytes 1572868
  118.0 298.1 %reduce-scatter.2.cloned.1.call-start = ((), (), s32[]{:S(2)}) async-start(), calls=%async_computation.3 | async-start | bytes 15728640 | tf_op jit(solution)/shard_map/reduce_scatter | solution.py:61
  206.9 209.2 %copy-start.1 = (f32[512,64]{0,1:T(8,128)S(1)}, f32[512,64]{0,1:T(8,128)}, u32[]{:S(2)}) copy-start(f32[512,64]{0,1:T(8,128)} %all-reduce.4.cloned.1.call-done) | copy-start | bytes 393220
Sparse Core Ops, SparseCore 0:
  20.9 20.5 all-reduce.3
  205.0 17.7 reduce-scatter.1
Sparse Core Ops, SparseCore 1:
  24.0 87.0 all-gather.4
  113.7 83.0 all-gather.2
  203.6 208.9 all-reduce.5
where the time goes:
time: 430 us; the launch traced here: 429 us
  waiting for transfers between devices  359 us (83%)
  matrix products  32.9 us (8%)
  between operations  21 us (5%)
  other arithmetic  12.8 us (3%)
    psum x1, waiting for transfers between devices, shards(): lax.psum((slot_mark[:, None, None] * term_a[None], slot_mark[:, None, Non...  196 us
    all_gather x1, waiting for transfers between devices, shards(): weight_piece = lax.all_gather(value_weight, 'dp', axis=0, tiled=True)  78.8 us
    all_gather x1, waiting for transfers between devices, shards(): adapter_slice = lax.all_gather(adapter_down_maps, 'dp', axis=0, tiled=True)  64.2 us
    psum x1, waiting for transfers between devices, shards(): backward_rank_term = lax.psum(contract_last(masked, up_matrix), 'tensor')  18.2 us
    dot_general x3, matrix products, contract_last(): lax.dot_general(left, right, (((1,), (1,)), ((), ())), preferred_element_...  15.5 us
  transfers between devices with their start and end apart: 5, of which 4 were waited for; matrix products, arithmetic and copies ran while one was open for 8% of the time, Pallas kernels for 0%

commit v1 on v0

v1 whole, which is shorter than its diff:
```python
import functools

import jax
import jax.numpy as jnp
from jax import lax
from jax.experimental import pallas as pl
from jax.experimental.pallas import tpu as pltpu
from jax.sharding import PartitionSpec as P

CHUNKS = (1, 1)


def dot(left, right, left_dim, right_dim):
    return lax.dot_general(
        left,
        right,
        (((left_dim,), (right_dim,)), ((), ())),
        preferred_element_type=jnp.float32,
    )


def swap_cores(x):
    n = lax.axis_size("tensor")
    return lax.ppermute(x, "tensor", [(i, n - 1 - i) for i in range(n)])


def exchange(x, mask):
    return lax.ppermute(x, "dp", [(i, i ^ mask) for i in range(lax.axis_size("dp"))])


def pick(pieces, index):
    result = pieces[0]
    for i in range(1, len(pieces)):
        result = jnp.where(index == i, pieces[i], result)
    return result


def place_kernel(plan, count, *refs):
    sources, outs, sems = refs[:-3], refs[-3:-1], refs[-1]
    half = count // 2
    key = lax.axis_index("dp") ^ (lax.axis_index("tensor") * half)
    copies = []
    for number, (source, slot, mask, start, rows) in enumerate(plan):
        block = key ^ mask
        for part in range(2):
            copy = pltpu.make_async_copy(
                sources[source].at[slot],
                outs[part].at[block % half, pl.ds(start, rows)],
                sems.at[number],
            )
            copies.append((block // half == part, copy))
    for here, copy in copies:
        pl.when(here)(copy.start)
    for here, copy in copies:
        pl.when(here)(copy.wait)


def place(plan, sources, count, rows, columns):
    shape = jax.ShapeDtypeStruct((count // 2, rows, columns), sources[0].dtype)
    return pl.pallas_call(
        functools.partial(place_kernel, plan, count),
        out_shape=(shape, shape),
        in_specs=[pl.BlockSpec(memory_space=pl.ANY)] * len(sources),
        out_specs=[pl.BlockSpec(memory_space=pltpu.VMEM)] * 2,
        scratch_shapes=[pltpu.SemaphoreType.DMA((len(plan),))],
        compiler_params=pltpu.CompilerParams(vmem_limit_bytes=32 * 1024 * 1024),
        cost_estimate=pl.CostEstimate(
            flops=0, bytes_accessed=4 * count * rows * columns, transcendentals=0
        ),
    )(*sources)


def gather_rows(piece):
    count = lax.axis_size("dp")
    rows, columns = piece.shape
    low_masks = []
    mask = 1
    while mask < count // 4:
        low_masks.append(mask)
        mask *= 2
    high_masks = (0, count // 4, count // 2, 3 * count // 4)
    blocks = [piece] + [exchange(piece, m) for m in high_masks[1:]]
    stack = jnp.stack(blocks)
    plan, sources = [], []
    cut = (rows // 2 + 15) // 16 * 16
    for part, (begin, end) in enumerate(((0, cut), (cut, rows))):
        held = stack[:, begin:end]
        masks = list(high_masks)
        order = low_masks if part == 0 else low_masks[::-1]
        for step, m in enumerate(order):
            other = exchange(held, m)
            other_masks = [k ^ m for k in masks]
            if step < len(order) - 1:
                held = jnp.concatenate([held, other])
                masks = masks + other_masks
        for array, array_masks in ((held, masks), (other, other_masks)):
            for slot, k in enumerate(array_masks):
                plan.append((len(sources), slot, k, begin, end - begin))
            sources.append(array)
    mine, other = place(tuple(plan), sources, count, rows, columns)
    return mine.reshape(count // 2 * rows, columns), other.reshape(count // 2 * rows, columns)


def prepare_kernel(
    devices_ref, adapter_ref, valid_ref, down_ref, up_ref, cotangent_ref,
    masked_ref, back_ref, up_out_ref, blocks_ref, shared_ref, ids_ref,
):
    count = lax.axis_size("dp")
    position = lax.axis_index("dp")
    tenant_count = devices_ref.shape[0]
    row_count = cotangent_ref.shape[0]
    _, rank, width = up_ref.shape
    zero = jnp.int32(0)
    end, own_id, first, valid, devices = zero, zero, zero, zero, zero
    ids = [zero] * count
    for slot in range(tenant_count):
        start = end
        end = end + devices_ref[slot]
        adapter = adapter_ref[slot]
        mine = jnp.logical_and(start <= position, position < end)
        own_id = jnp.where(mine, adapter, own_id)
        first = jnp.where(mine, start, first)
        valid = jnp.where(mine, valid_ref[slot], valid)
        devices = jnp.where(mine, devices_ref[slot], devices)
        for i in range(count):
            ids[i] = jnp.where(jnp.logical_and(start <= i, i < end), adapter, ids[i])
    for i in range(count):
        ids_ref[i] = ids[i]
    shared_ref[0] = (devices > 1).astype(jnp.int32)
    rows = lax.broadcasted_iota(jnp.int32, (row_count, width), 0)
    keep = (position - first) * row_count + rows < valid
    masked = jnp.where(keep, cotangent_ref[...], jnp.zeros_like(cotangent_ref[...]))
    masked_ref[...] = masked
    up = up_ref[own_id]
    up_out_ref[...] = up
    back_ref[...] = dot(up, masked, 1, 1)
    low_count = count // 4
    quarter = down_ref.shape[0] // 4
    total = down_ref.shape[1]
    base = lax.axis_index("tensor") * (2 * quarter)
    upper = down_ref[pl.ds(pl.multiple_of(base, quarter), quarter), :]
    lower = down_ref[pl.ds(pl.multiple_of(base + quarter, quarter), quarter), :]
    source = lax.broadcasted_iota(jnp.int32, (total, 2 * rank), 0)
    lane = lax.broadcasted_iota(jnp.int32, (total, 2 * rank), 1)
    for m in range(count):
        target = ids_ref[position ^ m] * rank + lane
        pick_upper = (source == target).astype(jnp.float32)
        pick_upper = jnp.where(lane < rank, pick_upper, 0.0).astype(jnp.bfloat16)
        pick_lower = (source + rank == target).astype(jnp.float32)
        pick_lower = jnp.where(lane >= rank, pick_lower, 0.0).astype(jnp.bfloat16)
        block = dot(upper, pick_upper, 1, 0) + dot(lower, pick_lower, 1, 0)
        blocks_ref[m % low_count, m // low_count] = block.astype(jnp.bfloat16)


def prepare(devices, adapter_of, valid, down_maps, up_maps, cotangent, count):
    rows, total = down_maps.shape
    rank = up_maps.shape[1]
    smem = pl.BlockSpec(memory_space=pltpu.SMEM)
    vmem = pl.BlockSpec(memory_space=pltpu.VMEM)
    return pl.pallas_call(
        prepare_kernel,
        out_shape=(
            jax.ShapeDtypeStruct(cotangent.shape, cotangent.dtype),
            jax.ShapeDtypeStruct((rank, cotangent.shape[0]), jnp.float32),
            jax.ShapeDtypeStruct(up_maps.shape[1:], up_maps.dtype),
            jax.ShapeDtypeStruct((count // 4, 4, rows // 4, 2 * rank), down_maps.dtype),
            jax.ShapeDtypeStruct((1,), jnp.int32),
        ),
        in_specs=[smem] * 3 + [vmem] * 3,
        out_specs=[vmem] * 4 + [smem],
        scratch_shapes=[pltpu.SMEM((count,), jnp.int32)],
        compiler_params=pltpu.CompilerParams(vmem_limit_bytes=32 * 1024 * 1024),
    )(devices, adapter_of, valid, down_maps, up_maps, cotangent)


def low_kernel(rank, mine_refs, other_refs, normed_ref, low_ref, down_ref, full_ref):
    count = lax.axis_size("dp")
    position = lax.axis_index("dp")
    tensor_part = lax.axis_index("tensor")
    low_count = count // 4
    quarter = mine_refs[0].shape[-2]
    for refs, part in ((mine_refs, tensor_part), (other_refs, 1 - tensor_part)):
        for h, ref in enumerate(refs):
            for l in range(low_count):
                source = position ^ (h * low_count + l)
                block = ref[l]
                for side in range(2):
                    start = pl.multiple_of((source * 4 + part * 2 + side) * quarter, quarter)
                    full_ref[pl.ds(start, quarter), :] = block[:, side * rank : (side + 1) * rank]
    half = full_ref.shape[0] // 2
    low_ref[...] = dot(normed_ref[...], full_ref[...], 1, 0).astype(jnp.bfloat16)
    down_ref[...] = full_ref[pl.ds(pl.multiple_of(tensor_part * half, half), half), :]


def low_rank_of(mine, other, normed, rank):
    row_count, model_width = normed.shape

    def kernel(*refs):
        low_kernel(rank, refs[0:4], refs[4:8], *refs[8:])

    return pl.pallas_call(
        kernel,
        out_shape=(
            jax.ShapeDtypeStruct((row_count, rank), jnp.bfloat16),
            jax.ShapeDtypeStruct((model_width // 2, rank), jnp.bfloat16),
        ),
        in_specs=[pl.BlockSpec(memory_space=pltpu.VMEM)] * 9,
        out_specs=[pl.BlockSpec(memory_space=pltpu.VMEM)] * 2,
        scratch_shapes=[pltpu.VMEM((model_width, rank), jnp.bfloat16)],
        compiler_params=pltpu.CompilerParams(vmem_limit_bytes=40 * 1024 * 1024),
    )(*mine, *other, normed)


def send_blocks(blocks):
    low_count = blocks.shape[0]
    got = [blocks[0]] + [exchange(blocks[l], l) for l in range(1, low_count)]
    rows = [jnp.stack([g[h] for g in got]) for h in range(4)]
    return [rows[0]] + [exchange(rows[h], h * low_count) for h in range(1, 4)]


def sum_single_run(term, position):
    count = lax.axis_size("dp")
    low_count, high_step = count // 4, count // 4
    low, high = position % low_count, position // high_step
    rows, columns = term.shape
    part = rows // low_count

    def row_part(index):
        return lax.dynamic_slice_in_dim(term, index * part, part, 0)

    total = row_part(low)
    for m in range(1, low_count):
        total = total + exchange(row_part(low ^ m), m)
    width = columns // 4

    def column_part(index):
        return lax.dynamic_slice_in_dim(total, index * width, width, 1)

    share = column_part(high)
    for m in range(1, 4):
        share = share + exchange(column_part(high ^ m), m * high_step)
    share = share.astype(jnp.bfloat16)
    got = [share] + [exchange(share, m * high_step) for m in range(1, 4)]
    strip = jnp.concatenate([pick(got, high ^ i) for i in range(4)], axis=1)
    got = [strip] + [exchange(strip, m) for m in range(1, low_count)]
    return jnp.concatenate([pick(got, low ^ i) for i in range(low_count)], axis=0)


def shards(
    normed,
    cotangent,
    value_weight,
    adapter_down_maps,
    adapter_up_maps,
    tenant_devices,
    adapter_of,
    valid_tokens,
):
    row_count, model_width = normed.shape
    rank = adapter_up_maps.shape[1]
    tenant_count = tenant_devices.shape[0]
    width = value_weight.shape[1]
    count = lax.axis_size("dp")
    half_width = model_width // 2
    tensor_part = lax.axis_index("tensor")
    position = lax.axis_index("dp")

    if value_weight.shape[0] % 64 == 0:
        masked, back_half, up_matrix, blocks, shared = prepare(
            tenant_devices, adapter_of, valid_tokens, adapter_down_maps, adapter_up_maps, cotangent, count
        )
        shared = shared[0] > 0
        scaled_t = (2.0 * (back_half + swap_cores(back_half))).astype(jnp.bfloat16)
        mine = send_blocks(blocks)
        other = swap_cores(jnp.stack(mine))
        low_rank, down_keep = low_rank_of(mine, [other[h] for h in range(4)], normed, rank)
    else:
        slot_ends = jnp.cumsum(tenant_devices)
        tenant_slot = jnp.sum((slot_ends <= position).astype(jnp.int32))
        picker = (jnp.arange(tenant_count, dtype=jnp.int32) == tenant_slot).astype(jnp.int32)
        first_device = jnp.sum(picker * (slot_ends - tenant_devices))
        adapter_index = jnp.sum(picker * adapter_of)
        valid_count = jnp.sum(picker * valid_tokens)
        shared = jnp.sum(picker * tenant_devices) > 1
        offsets = (position - first_device) * row_count + jnp.arange(row_count, dtype=jnp.int32)
        keep_rows = offsets < valid_count
        up_matrix = lax.dynamic_index_in_dim(adapter_up_maps, adapter_index, 0, keepdims=False)
        masked = jnp.where(keep_rows[:, None], cotangent, jnp.zeros_like(cotangent))
        back_half = dot(up_matrix, masked, 1, 1)
        scaled_t = (2.0 * (back_half + swap_cores(back_half))).astype(jnp.bfloat16)
        down_maps = lax.all_gather(adapter_down_maps, "dp", axis=0, tiled=True)
        down_map = lax.dynamic_slice_in_dim(down_maps, adapter_index * rank, rank, 1)
        down_keep = lax.dynamic_slice_in_dim(down_map, tensor_part * half_width, half_width, 0)
        low_rank = dot(normed, down_map, 1, 0).astype(jnp.bfloat16)
    masked_other = swap_cores(masked)
    normed_keep = lax.dynamic_slice_in_dim(normed, tensor_part * half_width, half_width, 1)
    normed_give = lax.dynamic_slice_in_dim(normed, (1 - tensor_part) * half_width, half_width, 1)
    term_a = dot(scaled_t, normed_keep, 1, 0)
    term_b = 2.0 * dot(low_rank, masked, 0, 0)

    terms = jnp.concatenate([term_a, term_b], axis=1)
    most = 9 * count // 16
    if count - most == tenant_count - 1:
        total = sum_single_run(jnp.where(shared, terms, 0.0), position)
        grads = jnp.where(shared, total.astype(jnp.float32), terms)
    else:
        slot_ends = jnp.cumsum(tenant_devices)
        tenant_slot = jnp.sum((slot_ends <= position).astype(jnp.int32))
        marks = (jnp.arange(tenant_count, dtype=jnp.int32) == tenant_slot).astype(jnp.float32)
        totals = lax.psum(marks[:, None, None] * terms[None], "dp")
        grads = lax.dynamic_index_in_dim(totals, tenant_slot, 0, keepdims=False)
    grad_a, grad_b = grads[None, :, :half_width], grads[None, :, half_width:]

    gradient = dot(scaled_t, down_keep, 0, 1)
    values = []
    start = 0
    for share in CHUNKS:
        columns = width * share // sum(CHUNKS)
        stop = start + columns
        mine, give = gather_rows(value_weight[:, start:stop])
        other = swap_cores(give)
        base = dot(normed_keep, mine, 1, 0) + dot(normed_give, give, 1, 0)
        extra = dot(low_rank, up_matrix[:, start:stop], 1, 0)
        values.append((base + 2.0 * extra).astype(jnp.bfloat16))
        gradient = gradient + dot(masked[:, start:stop], mine, 1, 1)
        gradient = gradient + dot(masked_other[:, start:stop], other, 1, 1)
        start = stop
    values = jnp.concatenate(values, axis=1)
    return (values, gradient.astype(jnp.bfloat16), grad_a, grad_b)


def solution(mesh):
    return jax.shard_map(
        shards,
        mesh=mesh,
        in_specs=(
            P(("groups", "dp"), None),
            P(("groups", "dp"), "tensor"),
            P("dp", "tensor"),
            P("dp", "groups"),
            P("groups", None, "tensor"),
            P("groups"),
            P("groups"),
            P("groups"),
        ),
        out_specs=(
            P(("groups", "dp"), "tensor"),
            P(("groups", "dp"), "tensor"),
            P(("groups", "dp"), None, "tensor"),
            P(("groups", "dp"), None, "tensor"),
        ),
        check_vma=False,
    )
```

time: 430 us -> 136 us (0.32)
  waiting for transfers between devices: 359 us -> 30.5 us
  starting transfers between devices: 0.2 us -> 51 us
  between operations: 21 us -> 1.79 us
  Pallas kernels: 0 us -> 16 us
  other arithmetic: 12.8 us -> 2.01 us
  matrix products: 32.9 us -> 23.7 us
  local copies, waits for them, and re-layouts: 3.56 us -> 10.6 us
    psum x2 -> x0, waiting for transfers between devices: 215 us -> none  [the longest x1 196 us: shards(): lax.psum((slot_mark[:, None, None] * term_a[None], slot_mark[:, None, Non...]
    all_gather x2 -> x0, waiting for transfers between devices: 143 us -> none  [the longest x1 78.8 us: shards(): weight_piece = lax.all_gather(value_weight, 'dp', axis=0, tiled=True)]
    ppermute x0 -> x37, starting transfers between devices: none -> 51 us  [the longest x32 50.2 us: exchange(): lax.ppermute(x, 'dp', [(i, i ^ mask) for i in range(lax.axis_size('dp'))])]
    ppermute x0 -> x37, waiting for transfers between devices: none -> 30.5 us  [the longest x32 30.5 us: exchange(): lax.ppermute(x, 'dp', [(i, i ^ mask) for i in range(lax.axis_size('dp'))])]
    pallas_call x0 -> x4, Pallas kernels: none -> 16 us  [the longest x2 11.5 us: place(): pl.pallas_call(functools.partial(place_kernel, plan, count), out_shape=(s...]
    dot_general x8 -> x13, matrix products: 32.9 us -> 23.7 us  [dot(): lax.dot_general(left, right, (((left_dim,), (right_dim,)), ((), ())), pre...]
    unnamed x6 -> x29, local copies, waits for them, and re-layouts: 0.02 us -> 7.06 us
    reduce_sum x4 -> x0, other arithmetic: 6.45 us -> none  [the longest x1 1.94 us: shards(): valid_count = jnp.sum(picker * valid_tokens)]
  transfers between devices with their start and end apart: 5 -> 37, of which waited for: 4 -> 15; matrix products, arithmetic and copies ran while one was open for 8% -> 18% of each run, Pallas kernels for 0% -> 12%
where the time goes in v1:
time: 136 us
  starting transfers between devices  51 us (38%)
  waiting for transfers between devices  30.5 us (22%)
  matrix products  23.7 us (17%)
  Pallas kernels  16 us (12%)
  local copies, waits for them, and re-layouts  10.6 us (8%)
  other arithmetic  2.01 us (1%)
  between operations  1.79 us (1%)
    ppermute x32, starting transfers between devices, exchange(): lax.ppermute(x, 'dp', [(i, i ^ mask) for i in range(lax.axis_size('dp'))])  50.2 us
    ppermute x32, waiting for transfers between devices, exchange(): lax.ppermute(x, 'dp', [(i, i ^ mask) for i in range(lax.axis_size('dp'))])  30.5 us
    dot_general x13, matrix products, dot(): lax.dot_general(left, right, (((left_dim,), (right_dim,)), ((), ())), pre...  23.7 us
    pallas_call x2, Pallas kernels, place(): pl.pallas_call(functools.partial(place_kernel, plan, count), out_shape=(s...  11.5 us
    unnamed x29, local copies, waits for them, and re-layouts  7.06 us
  transfers between devices with their start and end apart: 37, of which 15 were waited for; matrix products, arithmetic and copies ran while one was open for 18% of the time, Pallas kernels for 12%

profile of v1, /device:TPU:0, one launch (start us, length us, event | category | flops | bytes accessed | tf_op | source)
XLA Modules:
  0.0 135.6 jit_solution(13352612435092058318)
XLA Ops:
  2.4 5.0 %collective-permute-start.16 = (bf16[320,256]{1,0:T(8,128)(2,1)S(1)}, bf16[320,256]{1,0:T(8,128)(2,1)}, u32[]{:S(2)}, u32[]{:S(2)}) collective-permute-start(bf16[320,256]{1,0:T(8,128)(2,1)S(1)} %get-tuple-element.43), channel_id=1, source_target_pairs={{0,24},{2,26},{4,28},{6,30},{8,16},{10,18},{12,20},{14,22},{16,8},... | collective-permute-start | bytes 491528 | tf_op jit(solution)/shard_map/ppermute | solution.py:28
  13.1 2.5 %shard_map.112 = (bf16[512,512]{1,0:T(8,128)(2,1)S(1)}, f32[64,512]{1,0:T(8,128)S(1)}, bf16[64,512]{1,0:T(8,128)(2,1)S(1)}, bf16[4,4,80,128]{3,2,1,0:T(8,128)(2,1)S(1)}, s32[1]{0:T(128)}) custom-call(s32[8]{0:T(128)S(1)} %copy-done.3, s32[8]{0:T(128)S(1)} %copy-done.4, s32[8]{0:T(128)S(1)} %copy-done.5, bf16[320,512]{1,0:T(8,128)(2,1)S(1)} %copy-done.2, ...), custom_call_target="tpu_custom_call" | custom-call | tf_op jit(solution)/shard_map/pallas_call | solution.py:160
  15.6 2.7 %collective-permute-start.9 = (bf16[4,80,128]{2,1,0:T(8,128)(2,1)S(1)}, bf16[4,80,128]{2,1,0:T(8,128)(2,1)S(1)}, u32[]{:S(2)}, u32[]{:S(2)}) collective-permute-start(bf16[4,80,128]{2,1,0:T(8,128)(2,1)S(1)} %get-tuple-element.54), channel_id=1, source_target_pairs={{0,6},{2,4},{4,2},{6,0},{8,14},{10,12},{12,10},{14,8},{16,22},{18,... | collective-permute-start | bytes 245768 | tf_op jit(solution)/shard_map/ppermute | solution.py:28
  22.8 2.7 %collective-permute-done.7 = bf16[4,80,128]{2,1,0:T(8,128)(2,1)S(1)} collective-permute-done((bf16[4,80,128]{2,1,0:T(8,128)(2,1)S(1)}, bf16[4,80,128]{2,1,0:T(8,128)(2,1)S(1)}, u32[]{:S(2)}, u32[]{:S(2)}) %collective-permute-start.7) | collective-permute-done | bytes 81952 | tf_op jit(solution)/shard_map/ppermute | solution.py:28
  27.1 3.0 %collective-permute-start.11 = (bf16[4,80,128]{2,1,0:T(8,128)(2,1)S(1)}, bf16[4,80,128]{2,1,0:T(8,128)(2,1)S(1)}, u32[]{:S(2)}, u32[]{:S(2)}) collective-permute-start(bf16[4,80,128]{2,1,0:T(8,128)(2,1)S(1)} %pad_maximum_fusion.12), channel_id=1, source_target_pairs={{0,16},{2,18},{4,20},{6,22},{8,24},{10,26},{12,28},{14,30},{16,0},... | collective-permute-start | bytes 245768 | tf_op jit(solution)/shard_map/ppermute | solution.py:28
  30.4 3.6 %collective-permute-start.12 = (bf16[4,80,128]{2,1,0:T(8,128)(2,1)S(1)}, bf16[4,80,128]{2,1,0:T(8,128)(2,1)S(1)}, u32[]{:S(2)}, u32[]{:S(2)}) collective-permute-start(bf16[4,80,128]{2,1,0:T(8,128)(2,1)S(1)} %pad_maximum_fusion.13), channel_id=1, source_target_pairs={{0,24},{2,26},{4,28},{6,30},{8,16},{10,18},{12,20},{14,22},{16,8},... | collective-permute-start | bytes 245768 | tf_op jit(solution)/shard_map/ppermute | solution.py:28
  34.0 2.3 %fusion.4 = f32[64,2560]{1,0:T(8,128)S(1)} fusion(bf16[64,512]{1,0:T(8,128)(2,1)S(1)} %multiply_convert_fusion, bf16[512,5120]{1,0:T(8,128)(2,1)} %refs_8_.1, s32[]{:T(128)S(6)} %select_n.203), kind=kOutput, calls=%fused_computation.5 | convolution fusion | flops 167772160 | bytes 3342340 | tf_op jit(solution)/shard_map/dot_general | solution.py:14
  36.9 6.4 %collective-permute-start.1 = (bf16[320,256]{1,0:T(8,128)(2,1)}, bf16[320,256]{1,0:T(8,128)(2,1)S(1)}, u32[]{:S(2)}, u32[]{:S(2)}) collective-permute-start(bf16[320,256]{1,0:T(8,128)(2,1)} %get-tuple-element.44), channel_id=1, source_target_pairs={{0,16},{2,18},{4,20},{6,22},{8,24},{10,26},{12,28},{14,30},{16,0},... | collective-permute-start | bytes 491528 | tf_op jit(solution)/shard_map/ppermute | solution.py:28
  46.8 3.4 %collective-permute-done.1 = bf16[320,256]{1,0:T(8,128)(2,1)S(1)} collective-permute-done((bf16[320,256]{1,0:T(8,128)(2,1)}, bf16[320,256]{1,0:T(8,128)(2,1)S(1)}, u32[]{:S(2)}, u32[]{:S(2)}) %collective-permute-start.1) | collective-permute-done | bytes 163872 | tf_op jit(solution)/shard_map/ppermute | solution.py:28
  51.9 2.0 %shard_map.113 = (bf16[512,64]{1,0:T(8,128)(2,1)S(1)}, bf16[2560,64]{1,0:T(8,128)(2,1)S(1)}) custom-call(bf16[4,80,128]{2,1,0:T(8,128)(2,1)S(1)} %get-tuple-element.64.refs_0_, bf16[4,80,128]{2,1,0:T(8,128)(2,1)S(1)} %collective-permute-done.10.refs_1_, bf16[4,80,128]{2,1,0:T(8,128)(2,1)S(1)} %collective-permute-done.11.refs_2_, ...), custom_call_target="tpu_custom_call" | custom-call | tf_op jit(solution)/shard_map/pallas_call | solution.py:201
  57.3 3.2 %fusion.52 = f32[512,2560]{1,0:T(8,128)} fusion(bf16[64,512]{1,0:T(8,128)(2,1)S(1)} %multiply_convert_fusion, bf16[2560,64]{1,0:T(8,128)(2,1)S(1)} %get-tuple-element.23), kind=kOutput, calls=%fused_computation.89 | convolution fusion | flops 167772160 | bytes 5636096 | tf_op jit(solution)/shard_map/dot_general | solution.py:14
  63.1 3.8 %collective-permute-done.26 = f32[16,3072]{1,0:T(8,128)S(1)} collective-permute-done((f32[16,3072]{1,0:T(8,128)S(1)}, f32[16,3072]{1,0:T(8,128)S(1)}, u32[]{:S(2)}, u32[]{:S(2)}) %collective-permute-start.26) | collective-permute-done | bytes 196640 | tf_op jit(solution)/shard_map/ppermute | solution.py:28
  68.5 2.1 %collective-permute-start.30 = (f32[16,768]{1,0:T(8,128)S(1)}, f32[16,768]{1,0:T(8,128)S(1)}, u32[]{:S(2)}, u32[]{:S(2)}) collective-permute-start(f32[16,768]{1,0:T(8,128)S(1)} %get-tuple-element.57), channel_id=1, source_target_pairs={{0,24},{2,26},{4,28},{6,30},{8,16},{10,18},{12,20},{14,22},{16,8},... | collective-permute-start | bytes 147464 | tf_op jit(solution)/shard_map/ppermute | solution.py:28
  70.6 2.4 %collective-permute-start.28 = (f32[16,768]{1,0:T(8,128)S(1)}, f32[16,768]{1,0:T(8,128)S(1)}, u32[]{:S(2)}, u32[]{:S(2)}) collective-permute-start(f32[16,768]{1,0:T(8,128)S(1)} %get-tuple-element.56), channel_id=1, source_target_pairs={{0,8},{2,10},{4,12},{6,14},{8,0},{10,2},{12,4},{14,6},{16,24},{18,... | collective-permute-start | bytes 147464 | tf_op jit(solution)/shard_map/ppermute | solution.py:28
  76.0 1.8 %collective-permute-start.31 = (bf16[16,768]{1,0:T(8,128)(2,1)S(1)}, bf16[16,768]{1,0:T(8,128)(2,1)S(1)}, u32[]{:S(2)}, u32[]{:S(2)}) collective-permute-start(bf16[16,768]{1,0:T(8,128)(2,1)S(1)} %add_convert_fusion.1), channel_id=1, source_target_pairs={{0,24},{2,26},{4,28},{6,30},{8,16},{10,18},{12,20},{14,22},{16,8},... | collective-permute-start | bytes 73736 | tf_op jit(solution)/shard_map/ppermute | solution.py:28
  86.6 3.1 %collective-permute-done.34 = bf16[16,3072]{1,0:T(8,128)(2,1)S(1)} collective-permute-done((bf16[16,3072]{1,0:T(8,128)(2,1)S(1)}, bf16[16,3072]{1,0:T(8,128)(2,1)S(1)}, u32[]{:S(2)}, u32[]{:S(2)}) %collective-permute-start.34) | collective-permute-done | bytes 98336 | tf_op jit(solution)/shard_map/ppermute | solution.py:28
  91.2 8.6 %collective-permute-done.35 = bf16[16,3072]{1,0:T(8,128)(2,1)S(1)} collective-permute-done((bf16[16,3072]{1,0:T(8,128)(2,1)S(1)}, bf16[16,3072]{1,0:T(8,128)(2,1)S(1)}, u32[]{:S(2)}, u32[]{:S(2)}) %collective-permute-start.35) | collective-permute-done | bytes 98336 | tf_op jit(solution)/shard_map/ppermute | solution.py:28
  103.2 5.7 %shard_map.114 = (bf16[8,320,256]{2,1,0:T(8,128)(2,1)S(1)}, bf16[8,320,256]{2,1,0:T(8,128)(2,1)}) custom-call(bf16[8,160,256]{2,1,0:T(8,128)(2,1)S(1)} %pad_maximum_fusion.5.refs_0_, bf16[8,160,256]{2,1,0:T(8,128)(2,1)S(1)} %collective-permute-done.18.refs_1_, bf16[8,160,256]{2,1,0:T(8,128)(2,1)S(1)} %pad_maximum_fusion.6.refs_2_, ...), custom_call_target="tpu_custom_call" | custom-call | bytes 5242880 | tf_op jit(solution)/shard_map/pallas_call | solution.py:60
  108.9 2.2 %fusion = f32[512,256]{0,1:T(8,128)S(1)} fusion(bf16[2560,256]{1,0:T(8,128)(2,1)} %bitcast.26, bf16[512,5120]{1,0:T(8,128)(2,1)S(1)} %bitcast.62, s32[]{:T(128)S(6)} %select_n.204), kind=kOutput, calls=%fused_computation.1 | convolution fusion | flops 671088640 | bytes 4456452 | tf_op jit(solution)/shard_map/dot_general | solution.py:14
  111.2 3.3 %fusion.35 = f32[512,2560]{1,0:T(8,128)} fusion(bf16[2560,256]{1,0:T(8,128)(2,1)S(1)} %bitcast.63, bf16[512,512]{1,0:T(8,128)(2,1)S(1)} %get-tuple-element.24), kind=kOutput, calls=%fused_computation.36 | convolution fusion | flops 671088640 | bytes 6815744 | tf_op jit(solution)/shard_map/dot_general | solution.py:14
  115.6 5.8 %shard_map.111 = (bf16[8,320,256]{2,1,0:T(8,128)(2,1)S(1)}, bf16[8,320,256]{2,1,0:T(8,128)(2,1)}) custom-call(bf16[8,160,256]{2,1,0:T(8,128)(2,1)S(1)} %pad_maximum_fusion.2.refs_0_, bf16[8,160,256]{2,1,0:T(8,128)(2,1)S(1)} %collective-permute-done.4.refs_1_, bf16[8,160,256]{2,1,0:T(8,128)(2,1)S(1)} %pad_maximum_fusion.3.refs_2_, ...), custom_call_target="tpu_custom_call" | custom-call | bytes 5242880 | tf_op jit(solution)/shard_map/pallas_call | solution.py:60
  122.4 2.2 %fusion.2 = f32[512,256]{0,1:T(8,128)S(1)} fusion(bf16[2560,256]{1,0:T(8,128)(2,1)} %bitcast.5, bf16[512,5120]{1,0:T(8,128)(2,1)S(1)} %bitcast.62, s32[]{:T(128)S(6)} %select_n.204), kind=kOutput, calls=%fused_computation.3 | convolution fusion | flops 671088640 | bytes 4456452 | tf_op jit(solution)/shard_map/dot_general | solution.py:14
  127.5 2.6 %fusion.33 = f32[512,2560]{1,0:T(8,128)S(1)} fusion(bf16[2560,256]{1,0:T(8,128)(2,1)} %collective-permute-done.23, bf16[512,512]{1,0:T(8,128)(2,1)S(1)} %collective-permute-done.22), kind=kOutput, calls=%fused_computation.34 | convolution fusion | flops 671088640 | bytes 6815744 | tf_op jit(solution)/shard_map/dot_general | solution.py:14
  131.2 4.4 %add_convert_fusion = bf16[512,2560]{1,0:T(8,128)(2,1)} fusion(f32[512,2560]{1,0:T(8,128)S(1)} %bitcast.71, f32[512,2560]{1,0:T(8,128)S(1)} %fusion.33, f32[512,2560]{1,0:T(8,128)S(1)} %bitcast.73, f32[512,2560]{1,0:T(8,128)S(1)} %fusion.37, bf16[2560,256]{1,0:T(8,128)(2,1)} %collective-permute-done.24, bf16[512,512]{1,0:T(8,128)(2,1)S(1)} %collective-permute-done.22), kind=kOutput, calls=%fused_computation | convolution fusion | flops 677642240 | bytes 25165824 | tf_op jit(solution)/shard_map/dot_general | solution.py:14
  (133 shorter events, 48.9 us)
Async XLA Ops:
  2.4 40.9 %collective-permute-start.16 = (bf16[320,256]{1,0:T(8,128)(2,1)S(1)}, bf16[320,256]{1,0:T(8,128)(2,1)}, u32[]{:S(2)}, u32[]{:S(2)}) collective-permute-start(bf16[320,256]{1,0:T(8,128)(2,1)S(1)} %get-tuple-element.43), channel_id=1, source_target_pairs={{0,24},{2,26},{4,28},{6,30},{8,16},{10,18},{12,20},{14,22},{16,8},... | collective-permute-start | bytes 491528 | tf_op jit(solution)/shard_map/ppermute | solution.py:28
  7.5 35.9 %collective-permute-start.15 = (bf16[320,256]{1,0:T(8,128)(2,1)S(1)}, bf16[320,256]{1,0:T(8,128)(2,1)}, u32[]{:S(2)}, u32[]{:S(2)}) collective-permute-start(bf16[320,256]{1,0:T(8,128)(2,1)S(1)} %get-tuple-element.43), channel_id=1, source_target_pairs={{0,16},{2,18},{4,20},{6,22},{8,24},{10,26},{12,28},{14,30},{16,0},... | collective-permute-start | bytes 491528 | tf_op jit(solution)/shard_map/ppermute | solution.py:28
  7.5 36.0 %collective-permute-start.14 = (bf16[320,256]{1,0:T(8,128)(2,1)S(1)}, bf16[320,256]{1,0:T(8,128)(2,1)}, u32[]{:S(2)}, u32[]{:S(2)}) collective-permute-start(bf16[320,256]{1,0:T(8,128)(2,1)S(1)} %get-tuple-element.43), channel_id=1, source_target_pairs={{0,8},{2,10},{4,12},{6,14},{8,0},{10,2},{12,4},{14,6},{16,24},{18,... | collective-permute-start | bytes 491528 | tf_op jit(solution)/shard_map/ppermute | solution.py:28
  27.1 9.1 %collective-permute-start.11 = (bf16[4,80,128]{2,1,0:T(8,128)(2,1)S(1)}, bf16[4,80,128]{2,1,0:T(8,128)(2,1)S(1)}, u32[]{:S(2)}, u32[]{:S(2)}) collective-permute-start(bf16[4,80,128]{2,1,0:T(8,128)(2,1)S(1)} %pad_maximum_fusion.12), channel_id=1, source_target_pairs={{0,16},{2,18},{4,20},{6,22},{8,24},{10,26},{12,28},{14,30},{16,0},... | collective-permute-start | bytes 245768 | tf_op jit(solution)/shard_map/ppermute | solution.py:28
  36.3 8.9 %collective-permute-start.2 = (bf16[320,256]{1,0:T(8,128)(2,1)}, bf16[320,256]{1,0:T(8,128)(2,1)S(1)}, u32[]{:S(2)}, u32[]{:S(2)}) collective-permute-start(bf16[320,256]{1,0:T(8,128)(2,1)} %get-tuple-element.44), channel_id=1, source_target_pairs={{0,24},{2,26},{4,28},{6,30},{8,16},{10,18},{12,20},{14,22},{16,8},... | collective-permute-start | bytes 491528 | tf_op jit(solution)/shard_map/ppermute | solution.py:28
  36.9 13.3 %collective-permute-start.1 = (bf16[320,256]{1,0:T(8,128)(2,1)}, bf16[320,256]{1,0:T(8,128)(2,1)S(1)}, u32[]{:S(2)}, u32[]{:S(2)}) collective-permute-start(bf16[320,256]{1,0:T(8,128)(2,1)} %get-tuple-element.44), channel_id=1, source_target_pairs={{0,16},{2,18},{4,20},{6,22},{8,24},{10,26},{12,28},{14,30},{16,0},... | collective-permute-start | bytes 491528 | tf_op jit(solution)/shard_map/ppermute | solution.py:28
  43.3 8.4 %collective-permute-start = (bf16[320,256]{1,0:T(8,128)(2,1)}, bf16[320,256]{1,0:T(8,128)(2,1)S(1)}, u32[]{:S(2)}, u32[]{:S(2)}) collective-permute-start(bf16[320,256]{1,0:T(8,128)(2,1)} %get-tuple-element.44), channel_id=1, source_target_pairs={{0,8},{2,10},{4,12},{6,14},{8,0},{10,2},{12,4},{14,6},{16,24},{18,... | collective-permute-start | bytes 491528 | tf_op jit(solution)/shard_map/ppermute | solution.py:28
  43.4 84.1 %collective-permute-start.22 = (bf16[512,512]{1,0:T(8,128)(2,1)S(1)}, bf16[512,512]{1,0:T(8,128)(2,1)S(1)}, u32[]{:S(2)}, u32[]{:S(2)}) collective-permute-start(bf16[512,512]{1,0:T(8,128)(2,1)S(1)} %get-tuple-element.24), channel_id=1, source_target_pairs={{0,1},{1,0},{2,3},{3,2},{4,5},{5,4},{6,7},{7,6},{8,9},{9,8},{10,11... | collective-permute-start | bytes 1572872 | tf_op jit(solution)/shard_map/ppermute | solution.py:24
  43.5 8.4 %collective-permute-start.13 = (bf16[4,4,80,128]{3,2,1,0:T(8,128)(2,1)S(1)}, bf16[4,4,80,128]{3,2,1,0:T(8,128)(2,1)S(1)}, u32[]{:S(2)}, u32[]{:S(2)}) collective-permute-start(bf16[4,4,80,128]{3,2,1,0:T(8,128)(2,1)S(1)} %pad_maximum_fusion.8), channel_id=1, source_target_pairs={{0,1},{1,0},{2,3},{3,2},{4,5},{5,4},{6,7},{7,6},{8,9},{9,8},{10,11... | collective-permute-start | bytes 983048 | tf_op jit(solution)/shard_map/ppermute | solution.py:24
  45.2 15.3 %collective-permute-start.17 = (bf16[4,160,256]{2,1,0:T(8,128)(2,1)S(1)}, bf16[4,160,256]{2,1,0:T(8,128)(2,1)S(1)}, u32[]{:S(2)}, u32[]{:S(2)}) collective-permute-start(bf16[4,160,256]{2,1,0:T(8,128)(2,1)S(1)} %get-tuple-element.36), channel_id=1, source_target_pairs={{0,2},{2,0},{4,6},{6,4},{8,10},{10,8},{12,14},{14,12},{16,18},{18,... | collective-permute-start | bytes 983048 | tf_op jit(solution)/shard_map/ppermute | solution.py:28
  50.2 20.4 %collective-permute-start.19 = (bf16[4,160,256]{2,1,0:T(8,128)(2,1)S(1)}, bf16[4,160,256]{2,1,0:T(8,128)(2,1)S(1)}, u32[]{:S(2)}, u32[]{:S(2)}) collective-permute-start(bf16[4,160,256]{2,1,0:T(8,128)(2,1)S(1)} %get-tuple-element.35), channel_id=1, source_target_pairs={{0,4},{2,6},{4,0},{6,2},{8,12},{10,14},{12,8},{14,10},{16,20},{18,... | collective-permute-start | bytes 983048 | tf_op jit(solution)/shard_map/ppermute | solution.py:28
  54.6 7.1 %collective-permute-start.27 = (f32[16,3072]{1,0:T(8,128)S(1)}, f32[16,3072]{1,0:T(8,128)S(1)}, u32[]{:S(2)}, u32[]{:S(2)}) collective-permute-start(f32[16,3072]{1,0:T(8,128)S(1)} %get-tuple-element.31), channel_id=1, source_target_pairs={{0,6},{2,4},{4,2},{6,0},{8,14},{10,12},{12,10},{14,8},{16,22},{18,... | collective-permute-start | bytes 589832 | tf_op jit(solution)/shard_map/ppermute | solution.py:28
  55.9 11.1 %collective-permute-start.26 = (f32[16,3072]{1,0:T(8,128)S(1)}, f32[16,3072]{1,0:T(8,128)S(1)}, u32[]{:S(2)}, u32[]{:S(2)}) collective-permute-start(f32[16,3072]{1,0:T(8,128)S(1)} %get-tuple-element.32), channel_id=1, source_target_pairs={{0,4},{2,6},{4,0},{6,2},{8,12},{10,14},{12,8},{14,10},{16,20},{18,... | collective-permute-start | bytes 589832 | tf_op jit(solution)/shard_map/ppermute | solution.py:28
  60.6 7.8 %collective-permute-start.25 = (f32[16,3072]{1,0:T(8,128)S(1)}, f32[16,3072]{1,0:T(8,128)S(1)}, u32[]{:S(2)}, u32[]{:S(2)}) collective-permute-start(f32[16,3072]{1,0:T(8,128)S(1)} %get-tuple-element.30), channel_id=1, source_target_pairs={{0,2},{2,0},{4,6},{6,4},{8,10},{10,8},{12,14},{14,12},{16,18},{18,... | collective-permute-start | bytes 589832 | tf_op jit(solution)/shard_map/ppermute | solution.py:28
  61.8 17.3 %collective-permute-start.3 = (bf16[4,160,256]{2,1,0:T(8,128)(2,1)S(1)}, bf16[4,160,256]{2,1,0:T(8,128)(2,1)S(1)}, u32[]{:S(2)}, u32[]{:S(2)}) collective-permute-start(bf16[4,160,256]{2,1,0:T(8,128)(2,1)S(1)} %get-tuple-element.34), channel_id=1, source_target_pairs={{0,2},{2,0},{4,6},{6,4},{8,10},{10,8},{12,14},{14,12},{16,18},{18,... | collective-permute-start | bytes 983048 | tf_op jit(solution)/shard_map/ppermute | solution.py:28
  74.5 11.5 %collective-permute-start.5 = (bf16[4,160,256]{2,1,0:T(8,128)(2,1)S(1)}, bf16[4,160,256]{2,1,0:T(8,128)(2,1)S(1)}, u32[]{:S(2)}, u32[]{:S(2)}) collective-permute-start(bf16[4,160,256]{2,1,0:T(8,128)(2,1)S(1)} %get-tuple-element.33), channel_id=1, source_target_pairs={{0,4},{2,6},{4,0},{6,2},{8,12},{10,14},{12,8},{14,10},{16,20},{18,... | collective-permute-start | bytes 983048 | tf_op jit(solution)/shard_map/ppermute | solution.py:28
  81.7 21.4 %collective-permute-start.18 = (bf16[8,160,256]{2,1,0:T(8,128)(2,1)S(1)}, bf16[8,160,256]{2,1,0:T(8,128)(2,1)S(1)}, u32[]{:S(2)}, u32[]{:S(2)}) collective-permute-start(bf16[8,160,256]{2,1,0:T(8,128)(2,1)S(1)} %pad_maximum_fusion.5.refs_0_), channel_id=1, source_target_pairs={{0,4},{2,6},{4,0},{6,2},{8,12},{10,14},{12,8},{14,10},{16,20},{18,... | collective-permute-start | bytes 1966088 | tf_op jit(solution)/shard_map/ppermute | solution.py:28
  83.0 6.7 %collective-permute-start.34 = (bf16[16,3072]{1,0:T(8,128)(2,1)S(1)}, bf16[16,3072]{1,0:T(8,128)(2,1)S(1)}, u32[]{:S(2)}, u32[]{:S(2)}) collective-permute-start(bf16[16,3072]{1,0:T(8,128)(2,1)S(1)} %pad_maximum_fusion.9), channel_id=1, source_target_pairs={{0,6},{2,4},{4,2},{6,0},{8,14},{10,12},{12,10},{14,8},{16,22},{18,... | collective-permute-start | bytes 294920 | tf_op jit(solution)/shard_map/ppermute | solution.py:28
  84.5 15.3 %collective-permute-start.35 = (bf16[16,3072]{1,0:T(8,128)(2,1)S(1)}, bf16[16,3072]{1,0:T(8,128)(2,1)S(1)}, u32[]{:S(2)}, u32[]{:S(2)}) collective-permute-start(bf16[16,3072]{1,0:T(8,128)(2,1)S(1)} %pad_maximum_fusion.9), channel_id=1, source_target_pairs={{0,4},{2,6},{4,0},{6,2},{8,12},{10,14},{12,8},{14,10},{16,20},{18,... | collective-permute-start | bytes 294920 | tf_op jit(solution)/shard_map/ppermute | solution.py:28
  86.0 14.4 %collective-permute-start.36 = (bf16[16,3072]{1,0:T(8,128)(2,1)S(1)}, bf16[16,3072]{1,0:T(8,128)(2,1)S(1)}, u32[]{:S(2)}, u32[]{:S(2)}) collective-permute-start(bf16[16,3072]{1,0:T(8,128)(2,1)S(1)} %pad_maximum_fusion.9), channel_id=1, source_target_pairs={{0,2},{2,0},{4,6},{6,4},{8,10},{10,8},{12,14},{14,12},{16,18},{18,... | collective-permute-start | bytes 294920 | tf_op jit(solution)/shard_map/ppermute | solution.py:28
  89.7 13.5 %collective-permute-start.20 = (bf16[8,160,256]{2,1,0:T(8,128)(2,1)S(1)}, bf16[8,160,256]{2,1,0:T(8,128)(2,1)S(1)}, u32[]{:S(2)}, u32[]{:S(2)}) collective-permute-start(bf16[8,160,256]{2,1,0:T(8,128)(2,1)S(1)} %pad_maximum_fusion.6.refs_2_), channel_id=1, source_target_pairs={{0,2},{2,0},{4,6},{6,4},{8,10},{10,8},{12,14},{14,12},{16,18},{18,... | collective-permute-start | bytes 1966088 | tf_op jit(solution)/shard_map/ppermute | solution.py:28
  99.8 14.6 %collective-permute-start.4 = (bf16[8,160,256]{2,1,0:T(8,128)(2,1)S(1)}, bf16[8,160,256]{2,1,0:T(8,128)(2,1)S(1)}, u32[]{:S(2)}, u32[]{:S(2)}) collective-permute-start(bf16[8,160,256]{2,1,0:T(8,128)(2,1)S(1)} %pad_maximum_fusion.2.refs_0_), channel_id=1, source_target_pairs={{0,4},{2,6},{4,0},{6,2},{8,12},{10,14},{12,8},{14,10},{16,20},{18,... | collective-permute-start | bytes 1966088 | tf_op jit(solution)/shard_map/ppermute | solution.py:28
  100.3 15.2 %collective-permute-start.6 = (bf16[8,160,256]{2,1,0:T(8,128)(2,1)S(1)}, bf16[8,160,256]{2,1,0:T(8,128)(2,1)S(1)}, u32[]{:S(2)}, u32[]{:S(2)}) collective-permute-start(bf16[8,160,256]{2,1,0:T(8,128)(2,1)S(1)} %pad_maximum_fusion.3.refs_2_), channel_id=1, source_target_pairs={{0,2},{2,0},{4,6},{6,4},{8,10},{10,8},{12,14},{14,12},{16,18},{18,... | collective-permute-start | bytes 1966088 | tf_op jit(solution)/shard_map/ppermute | solution.py:28
  108.8 21.3 %collective-permute-start.24 = (bf16[2560,256]{1,0:T(8,128)(2,1)}, bf16[2560,256]{1,0:T(8,128)(2,1)}, u32[]{:S(2)}, u32[]{:S(2)}) collective-permute-start(bf16[2560,256]{1,0:T(8,128)(2,1)} %bitcast.26), channel_id=1, source_target_pairs={{0,1},{1,0},{2,3},{3,2},{4,5},{5,4},{6,7},{7,6},{8,9},{9,8},{10,11... | collective-permute-start | bytes 3932168 | tf_op jit(solution)/shard_map/ppermute | solution.py:24
  (27 other events, 190.4 us)

commit v2 on v0

v2 whole, which is shorter than its diff:
```python
import functools

import jax
import jax.numpy as jnp
from jax import lax
from jax.experimental import pallas as pl
from jax.experimental.pallas import tpu as pltpu
from jax.sharding import PartitionSpec as P

EXCHANGED = (1, 2)

HBM = pl.BlockSpec(memory_space=pltpu.HBM)
VMEM = pl.BlockSpec(memory_space=pltpu.VMEM)
SMEM = pl.BlockSpec(memory_space=pltpu.SMEM)


SHORT = pl.CostEstimate(flops=1, bytes_accessed=1, transcendentals=0)


def vmem_limit(mib):
    return pltpu.CompilerParams(vmem_limit_bytes=mib * 1024 * 1024)


def dot(left, right, left_dim, right_dim):
    return lax.dot_general(
        left,
        right,
        (((left_dim,), (right_dim,)), ((), ())),
        preferred_element_type=jnp.float32,
    )


def swap_cores(x):
    n = lax.axis_size("tensor")
    return lax.ppermute(x, "tensor", [(i, n - 1 - i) for i in range(n)])


def exchange(x, mask):
    return lax.ppermute(x, "dp", [(i, i ^ mask) for i in range(lax.axis_size("dp"))])


def pick(pieces, index):
    result = pieces[0]
    for i in range(1, len(pieces)):
        result = jnp.where(index == i, pieces[i], result)
    return result


def fence(x, *others):
    def kernel(*refs):
        pass

    return pl.pallas_call(
        kernel,
        out_shape=jax.ShapeDtypeStruct(x.shape, x.dtype),
        in_specs=[HBM] * (1 + len(others)),
        out_specs=HBM,
        input_output_aliases={0: 0},
        cost_estimate=SHORT,
    )(x, *others)


def kernel_call(body, ins, outs, scalars=(), raw=(), scratch=()):
    counts = (len(scalars), len(ins), len(raw), len(outs), len(ins), len(outs), len(scratch), 1)

    def kernel(*refs):
        groups, start = [], 0
        for count in counts:
            groups.append(refs[start : start + count])
            start += count
        scalar_refs, in_hbm, raw_refs, out_hbm, in_refs, out_refs, scratch_refs, (sems,) = groups
        loads = [
            pltpu.make_async_copy(source, target, sems.at[i])
            for i, (source, target) in enumerate(zip(in_hbm, in_refs))
        ]
        for load in loads:
            load.start()
        stores = []

        def get(i):
            loads[i].wait()
            return in_refs[i]

        def put(i):
            store = pltpu.make_async_copy(out_refs[i], out_hbm[i], sems.at[len(ins) + i])
            store.start()
            stores.append(store)

        body(scalar_refs, get, raw_refs, out_refs, put, scratch_refs)
        for store in stores:
            store.wait()

    return pl.pallas_call(
        kernel,
        out_shape=tuple(outs),
        in_specs=[SMEM] * len(scalars) + [HBM] * (len(ins) + len(raw)),
        out_specs=tuple([HBM] * len(outs)),
        scratch_shapes=[
            *[pltpu.VMEM(x.shape, x.dtype) for x in (*ins, *outs)],
            *scratch,
            pltpu.SemaphoreType.DMA((len(ins) + len(outs),)),
        ],
        compiler_params=vmem_limit(56),
        cost_estimate=SHORT,
    )(*scalars, *ins, *raw)


def high_masks():
    step = lax.axis_size("dp") // 4
    return (0, step, 2 * step, 3 * step)


def low_masks():
    masks, mask = [], 1
    while mask < lax.axis_size("dp") // 4:
        masks.append(mask)
        mask *= 2
    return masks


def first_phase(piece):
    low_count = lax.axis_size("dp") // 4
    slots = []
    for r in range(4):
        pairs = []
        for z in range(4):
            for t in range(2):
                source = 2 * t + (z ^ r) % 2
                core = (z ^ r) // 2
                for low in range(low_count):
                    pairs.append(((source * low_count + low) * 2 + core, (z * low_count + low) * 2 + t))
        slots.append(lax.ppermute(piece, ("dp", "tensor"), pairs))
    return slots


def row_parts(slots):
    rows = slots[0].shape[0]
    cut = (rows // 2 + 15) // 16 * 16
    return [jnp.stack([x[:cut] for x in slots]), jnp.stack([x[cut:] for x in slots])]


def middle_phases(parts):
    arrays, masks, last = [], [], []
    for part, held in enumerate(parts):
        order = low_masks() if part == 0 else low_masks()[::-1]
        own = [0]
        for m in order[:-1]:
            held = jnp.concatenate([held, exchange(held, m)])
            own = own + [k ^ m for k in own]
        arrays.append(held)
        masks.append(own)
        last.append(order[-1])
    return arrays, masks, last


def last_phase(arrays, masks, last):
    got = [exchange(x, m) for x, m in zip(arrays, last)]
    entries, begin = [], 0
    for part, held in enumerate(arrays):
        rows = held.shape[1]
        for number, flip in ((part, 0), (part + 2, last[part])):
            for slot in range(held.shape[0]):
                entries.append((number, slot, masks[part][slot // 4] ^ flip, slot % 4, begin, rows))
        begin += rows
    return got, tuple(entries)


def forward(arrays, plan, normed, low_rank, mine, begin, columns):
    count = lax.axis_size("dp")
    half, step = count // 2, count // 4
    row_count, half_width = normed.shape[0], normed.shape[1] // 2
    rows = half_width // half

    def body(scalars, get, raw, outs, put, scratch):
        own_ref, theirs_ref, weight_ref = outs
        normed_ref, sems = scratch
        position, tensor_part = lax.axis_index("dp"), lax.axis_index("tensor")
        top = position // half
        start = pl.multiple_of(tensor_part * half_width, half_width)
        copies = [
            pltpu.make_async_copy(raw[-1].at[:, pl.ds(start, half_width)], normed_ref, sems.at[len(plan)])
        ]
        for number, (source, slot, mask, r, first, size) in enumerate(plan):
            block = (position ^ (mask + (r % 2) * step)) % half
            copies.append(
                pltpu.make_async_copy(
                    raw[source].at[slot],
                    weight_ref.at[top ^ (r // 2), block, pl.ds(first, size)],
                    sems.at[number],
                )
            )
        for copy in copies:
            copy.start()
        up = get(1)[row_count:, begin : begin + columns]
        extra = 2.0 * dot(get(0)[...], up, 1, 0)
        for copy in copies:
            copy.wait()
        put(2)
        theirs_ref[...] = dot(normed_ref[...], weight_ref[1 - tensor_part].reshape(half_width, columns), 1, 0)
        put(1)
        own_ref[...] = extra + dot(normed_ref[...], weight_ref[tensor_part].reshape(half_width, columns), 1, 0)
        put(0)

    partial = jax.ShapeDtypeStruct((row_count, columns), jnp.float32)
    return kernel_call(
        body,
        (low_rank, mine),
        (partial, partial, jax.ShapeDtypeStruct((2, half, rows, columns), jnp.bfloat16)),
        raw=(*arrays, normed),
        scratch=(
            pltpu.VMEM((row_count, half_width), jnp.bfloat16),
            pltpu.SemaphoreType.DMA((len(plan) + 1,)),
        ),
    )


def tile_blocks(rows, half):
    blocks = 1
    while blocks < half and (blocks * rows < 512 or blocks * rows % 128):
        blocks *= 2
    return blocks


def gradient_kernel(part_ref, weight_ref, gathered_ref, mine_ref, other_ref, scaled_ref, down_ref, out_ref):
    tensor_part = part_ref[0]
    _, blocks, rows, cut = weight_ref.shape
    size, columns = blocks * rows, gathered_ref.shape[3]
    total = dot(scaled_ref[...], down_ref[...], 0, 1)
    for ref, core in ((mine_ref, tensor_part), (other_ref, 1 - tensor_part)):
        total = total + dot(ref[:, :cut], weight_ref[core].reshape(size, cut), 1, 1)
        total = total + dot(ref[:, cut:], gathered_ref[:, core].reshape(size, columns), 1, 1)
    out_ref[...] = total.astype(out_ref.dtype)


def input_gradient(part, weight, gathered, mine, other, scaled_t, down_keep):
    _, half, rows, cut = weight.shape
    columns = gathered.shape[3]
    rank, row_count = scaled_t.shape
    blocks = tile_blocks(rows, half)
    width, steps = blocks * rows, half // blocks
    masked = pl.BlockSpec((row_count, mine.shape[1]), lambda i, part: (0, 0))
    return pl.pallas_call(
        gradient_kernel,
        grid_spec=pltpu.PrefetchScalarGridSpec(
            num_scalar_prefetch=1,
            grid=(steps,),
            in_specs=[
                pl.BlockSpec((2, blocks, rows, cut), lambda i, part: (0, i, 0, 0)),
                pl.BlockSpec((blocks, 2, rows, columns), lambda i, part: (part[0] * steps + i, 0, 0, 0)),
                masked,
                masked,
                pl.BlockSpec((rank, row_count), lambda i, part: (0, 0)),
                pl.BlockSpec((width, rank), lambda i, part: (i, 0)),
            ],
            out_specs=pl.BlockSpec((row_count, width), lambda i, part: (0, i)),
        ),
        out_shape=jax.ShapeDtypeStruct((row_count, width * steps), jnp.bfloat16),
        compiler_params=vmem_limit(56),
        cost_estimate=SHORT,
    )(part, weight, gathered, mine, other, scaled_t, down_keep)


def last_values_kernel(part_ref, weight_ref, normed_ref, low_ref, up_ref, first_ref, out_ref, total_ref):
    step = pl.program_id(0)
    blocks, _, rows, columns = weight_ref.shape
    begin = first_ref.shape[1]
    row_count = low_ref.shape[0]

    @pl.when(step == 0)
    def _():
        out_ref[:, :begin] = first_ref[...]
        total_ref[...] = 2.0 * dot(low_ref[...], up_ref[row_count:, begin:], 1, 0)

    total_ref[...] += dot(normed_ref[...], weight_ref[...].reshape(blocks * rows, columns), 1, 0)

    @pl.when(step == pl.num_programs(0) - 1)
    def _():
        out_ref[:, begin:] = total_ref[...].astype(out_ref.dtype)


def last_values(part, gathered, normed, low_rank, mine, first):
    count, _, rows, columns = gathered.shape
    row_count = normed.shape[0]
    blocks = 2 * tile_blocks(rows, count // 2)
    width = blocks * rows

    def whole(x):
        return pl.BlockSpec(x.shape, lambda i, part: (0, 0))

    return pl.pallas_call(
        last_values_kernel,
        grid_spec=pltpu.PrefetchScalarGridSpec(
            num_scalar_prefetch=1,
            grid=(count // blocks,),
            in_specs=[
                pl.BlockSpec((blocks, 1, rows, columns), lambda i, part: (i, part[0], 0, 0)),
                pl.BlockSpec((row_count, width), lambda i, part: (0, i)),
                whole(low_rank),
                whole(mine),
                whole(first),
            ],
            out_specs=pl.BlockSpec((row_count, first.shape[1] + columns), lambda i, part: (0, 0)),
            scratch_shapes=[pltpu.VMEM((row_count, columns), jnp.float32)],
        ),
        out_shape=jax.ShapeDtypeStruct((row_count, first.shape[1] + columns), jnp.bfloat16),
        compiler_params=vmem_limit(56),
        cost_estimate=SHORT,
    )(part, gathered, normed, low_rank, mine, first)


def prepare_kernel(
    devices_ref, adapter_ref, valid_ref, down_hbm, up_hbm, cotangent_hbm,
    mine_ref, shared_ref, *refs,
):
    block_refs, (ids_ref, down_ref, cotangent_ref, sems) = refs[:-4], refs[-4:]
    count = lax.axis_size("dp")
    position = lax.axis_index("dp")
    tenant_count = devices_ref.shape[0]
    row_count, width = cotangent_ref.shape
    rank = mine_ref.shape[0] - row_count
    half_rows, total = down_ref.shape
    quarter = half_rows // 2
    low_count = count // 4
    base = pl.multiple_of(lax.axis_index("tensor") * half_rows, half_rows)
    load_cotangent = pltpu.make_async_copy(cotangent_hbm, cotangent_ref, sems.at[0])
    load_down = pltpu.make_async_copy(down_hbm.at[pl.ds(base, half_rows)], down_ref, sems.at[1])
    load_cotangent.start()
    load_down.start()
    zero = jnp.int32(0)
    end, own_id, first, valid, devices = zero, zero, zero, zero, zero
    ids = [zero] * count
    for slot in range(tenant_count):
        start = end
        end = end + devices_ref[slot]
        adapter = adapter_ref[slot]
        mine = jnp.logical_and(start <= position, position < end)
        own_id = jnp.where(mine, adapter, own_id)
        first = jnp.where(mine, start, first)
        valid = jnp.where(mine, valid_ref[slot], valid)
        devices = jnp.where(mine, devices_ref[slot], devices)
        for i in range(count):
            ids[i] = jnp.where(jnp.logical_and(start <= i, i < end), adapter, ids[i])
    for i in range(count):
        ids_ref[i] = ids[i]
    load_up = pltpu.make_async_copy(up_hbm.at[own_id], mine_ref.at[pl.ds(row_count, rank)], sems.at[2])
    load_up.start()
    shared_ref[0] = (devices > 1).astype(jnp.int32)
    rows = lax.broadcasted_iota(jnp.int32, (row_count, width), 0)
    keep = (position - first) * row_count + rows < valid
    load_cotangent.wait()
    mine_ref[:row_count, :] = jnp.where(keep, cotangent_ref[...], jnp.zeros_like(cotangent_ref[...]))
    load_down.wait()
    upper, lower = down_ref[0:quarter, :], down_ref[quarter:half_rows, :]
    source = lax.broadcasted_iota(jnp.int32, (total, 2 * rank), 0)
    lane = lax.broadcasted_iota(jnp.int32, (total, 2 * rank), 1) % rank
    first_side = lax.broadcasted_iota(jnp.int32, (quarter, 2 * rank), 1) < rank
    for m in range(count):
        chosen = (source == ids_ref[position ^ m] * rank + lane).astype(jnp.float32).astype(jnp.bfloat16)
        block = jnp.where(first_side, dot(upper, chosen, 1, 0), dot(lower, chosen, 1, 0))
        block_refs[m % low_count][m // low_count] = block.astype(jnp.bfloat16)
    load_up.wait()


def prepare(devices, adapter_of, valid, down_maps, up_maps, cotangent, count):
    rows, total = down_maps.shape
    rank = up_maps.shape[1]
    row_count, width = cotangent.shape
    return pl.pallas_call(
        prepare_kernel,
        out_shape=(
            jax.ShapeDtypeStruct((row_count + rank, width), cotangent.dtype),
            jax.ShapeDtypeStruct((1,), jnp.int32),
            *[jax.ShapeDtypeStruct((4, rows // 4, 2 * rank), down_maps.dtype)] * (count // 4),
        ),
        in_specs=[SMEM] * 3 + [HBM] * 3,
        out_specs=[VMEM, SMEM] + [VMEM] * (count // 4),
        scratch_shapes=[
            pltpu.SMEM((count,), jnp.int32),
            pltpu.VMEM((rows // 2, total), down_maps.dtype),
            pltpu.VMEM(cotangent.shape, cotangent.dtype),
            pltpu.SemaphoreType.DMA((3,)),
        ],
        compiler_params=vmem_limit(60),
        cost_estimate=SHORT,
    )(devices, adapter_of, valid, down_maps, up_maps, cotangent)


def back(mine, other, normed):
    row_count, half_width = normed.shape[0], normed.shape[1] // 2
    rank = mine.shape[0] - row_count

    def body(scalars, get, raw, outs, put, scratch):
        scaled_ref, term_ref = outs
        normed_ref, sem = scratch
        start = pl.multiple_of(lax.axis_index("tensor") * half_width, half_width)
        load = pltpu.make_async_copy(raw[0].at[:, pl.ds(start, half_width)], normed_ref, sem)
        load.start()
        mine_ref, other_ref = get(0), get(1)
        total = dot(mine_ref[row_count:, :], mine_ref[:row_count, :], 1, 1)
        total = total + dot(other_ref[row_count:, :], other_ref[:row_count, :], 1, 1)
        scaled = (2.0 * total).astype(jnp.bfloat16)
        scaled_ref[...] = scaled
        put(0)
        load.wait()
        term_ref[...] = dot(scaled, normed_ref[...], 1, 0)
        put(1)

    return kernel_call(
        body,
        (mine, other),
        (
            jax.ShapeDtypeStruct((rank, row_count), jnp.bfloat16),
            jax.ShapeDtypeStruct((rank, half_width), jnp.float32),
        ),
        raw=(normed,),
        scratch=(pltpu.VMEM((row_count, half_width), jnp.bfloat16), pltpu.SemaphoreType.DMA),
    )


def low_rank_of(shared, own, other, mine, term_a, normed, rank, *others, pieces=4):
    row_count, model_width = normed.shape
    half_width = model_width // 2
    columns = mine.shape[1]
    count = lax.axis_size("dp")
    low_count = count // 4
    quarter = own.shape[-2]
    size = rank // low_count
    piece = model_width // pieces

    def body(scalars, get, raw, outs, put, scratch):
        low_ref, down_ref, term_ref, *part_refs = outs
        full_ref, normed_ref, total_ref, sems = scratch
        position, tensor_part = lax.axis_index("dp"), lax.axis_index("tensor")
        loads = []
        for i in range(pieces):
            lanes = pl.ds(i * piece, piece)
            loads.append(pltpu.make_async_copy(raw[0].at[:, lanes], normed_ref.at[:, lanes], sems.at[i]))
        for load in loads:
            load.start()
        for ref, part in ((get(0), tensor_part), (get(1), 1 - tensor_part)):
            for h in range(4):
                for l in range(low_count):
                    source = position ^ (h * low_count + l)
                    block = ref[h, l]
                    for side in range(2):
                        start = pl.multiple_of((source * 4 + part * 2 + side) * quarter, quarter)
                        full_ref[pl.ds(start, quarter), :] = block[:, side * rank : (side + 1) * rank]
        down_ref[...] = full_ref[pl.ds(pl.multiple_of(tensor_part * half_width, half_width), half_width), :]
        put(1)
        for i, load in enumerate(loads):
            load.wait()
            rows = slice(i * piece, (i + 1) * piece)
            product = dot(normed_ref[:, rows], full_ref[rows, :], 1, 0)
            total_ref[...] = product if i == 0 else total_ref[...] + product
        low = total_ref[...].astype(jnp.bfloat16)
        low_ref[...] = low
        put(0)
        term_ref[...] = 2.0 * dot(low, get(2)[:row_count, :], 0, 0)
        put(2)
        shared_here = scalars[0][0] > 0
        a_ref = get(3)
        for m, ref in enumerate(part_refs):
            start = pl.multiple_of(((position % low_count) ^ m) * size, size)
            ref[:, :half_width] = jnp.where(shared_here, a_ref[pl.ds(start, size), :], 0.0)
            ref[:, half_width:] = jnp.where(shared_here, term_ref[pl.ds(start, size), :], 0.0)
            put(3 + m)

    part = jax.ShapeDtypeStruct((size, half_width + columns), jnp.float32)
    result = kernel_call(
        body,
        (own, other, mine, term_a),
        (
            jax.ShapeDtypeStruct((row_count, rank), jnp.bfloat16),
            jax.ShapeDtypeStruct((half_width, rank), jnp.bfloat16),
            jax.ShapeDtypeStruct((rank, columns), jnp.float32),
            *[part] * low_count,
        ),
        scalars=(shared,),
        raw=(normed, *others),
        scratch=(
            pltpu.VMEM((model_width, rank), jnp.bfloat16),
            pltpu.VMEM((row_count, model_width), jnp.bfloat16),
            pltpu.VMEM((row_count, rank), jnp.float32),
            pltpu.SemaphoreType.DMA((pieces,)),
        ),
    )
    return result[0], result[1], result[2], result[3:]


def send_blocks_low(blocks):
    got = [blocks[0]] + [exchange(block, l) for l, block in enumerate(blocks) if l]

    def body(scalars, get, raw, outs, put, scratch):
        refs = [get(l) for l in range(len(got))]
        for h, out in enumerate(outs):
            for l, ref in enumerate(refs):
                out[l] = ref[h]
            put(h)

    shape = jax.ShapeDtypeStruct((len(got),) + got[0].shape[1:], got[0].dtype)
    return list(kernel_call(body, got, [shape] * 4))


def send_blocks_high(rows):
    return jnp.stack([rows[0]] + [exchange(row, m) for row, m in zip(rows[1:], high_masks()[1:])])


def row_sums(parts):
    total = parts[0]
    for m, part in enumerate(parts):
        if m:
            total = total + exchange(part, m)
    return total


def sum_to_strip(total):
    low_count = lax.axis_size("dp") // 4
    high = lax.axis_index("dp") // low_count
    width = total.shape[1] // 4

    def column_part(index):
        return lax.dynamic_slice_in_dim(total, index * width, width, 1)

    share = column_part(high)
    for m in range(1, 4):
        share = share + exchange(column_part(high ^ m), m * low_count)
    share = share.astype(jnp.bfloat16)
    got = [share] + [exchange(share, m * low_count) for m in range(1, 4)]
    return jnp.concatenate([pick(got, high ^ i) for i in range(4)], axis=1)


def gather_strips(strip):
    low_count = lax.axis_size("dp") // 4
    low = lax.axis_index("dp") % low_count
    got = [strip] + [exchange(strip, m) for m in range(1, low_count)]
    return jnp.concatenate([pick(got, low ^ i) for i in range(low_count)], axis=0)


def shards(
    normed,
    cotangent,
    value_weight,
    adapter_down_maps,
    adapter_up_maps,
    tenant_devices,
    adapter_of,
    valid_tokens,
):
    row_count, model_width = normed.shape
    rank = adapter_up_maps.shape[1]
    tenant_count = tenant_devices.shape[0]
    width = value_weight.shape[1]
    count = lax.axis_size("dp")
    half_width = model_width // 2
    tensor_part = lax.axis_index("tensor")
    position = lax.axis_index("dp")
    cut = width * EXCHANGED[0] // EXCHANGED[1]

    slots = first_phase(value_weight[:, :cut])
    gathered = lax.all_gather(value_weight[:, cut:], ("dp", "tensor"), axis=0)
    gathered = gathered.reshape(count, 2, value_weight.shape[0], width - cut)

    most = 9 * count // 16
    single_run = count - most == tenant_count - 1
    if value_weight.shape[0] % 64 == 0 and single_run:
        mine, shared, *blocks = prepare(
            tenant_devices, adapter_of, valid_tokens, adapter_down_maps, adapter_up_maps, cotangent, count
        )
        other = swap_cores(mine)
        scaled_t, term_a = back(mine, other, normed)
        rows = send_blocks_low(blocks)
        held, masks, last = middle_phases(row_parts(slots))
        own_blocks = send_blocks_high(rows)
        low_rank, down_keep, term_b, parts = low_rank_of(
            shared, own_blocks, swap_cores(own_blocks), mine, term_a, normed, rank
        )
        got, plan = last_phase(held, masks, last)
        strip = sum_to_strip(row_sums(parts))
        total = gather_strips(fence(strip, gathered)).astype(jnp.float32)
        grad_a = jnp.where(shared[0] > 0, total[:, :half_width], term_a)[None]
        grad_b = jnp.where(shared[0] > 0, total[:, half_width:], term_b)[None]
    else:
        slot_ends = jnp.cumsum(tenant_devices)
        tenant_slot = jnp.sum((slot_ends <= position).astype(jnp.int32))
        picker = (jnp.arange(tenant_count, dtype=jnp.int32) == tenant_slot).astype(jnp.int32)
        first_device = jnp.sum(picker * (slot_ends - tenant_devices))
        adapter_index = jnp.sum(picker * adapter_of)
        valid_count = jnp.sum(picker * valid_tokens)
        offsets = (position - first_device) * row_count + jnp.arange(row_count, dtype=jnp.int32)
        keep_rows = offsets < valid_count
        up_matrix = lax.dynamic_index_in_dim(adapter_up_maps, adapter_index, 0, keepdims=False)
        masked = jnp.where(keep_rows[:, None], cotangent, jnp.zeros_like(cotangent))
        mine = jnp.concatenate([masked, up_matrix])
        other = swap_cores(mine)
        scaled_t, term_a = back(mine, other, normed)
        down_maps = lax.all_gather(adapter_down_maps, "dp", axis=0, tiled=True)
        down_map = lax.dynamic_slice_in_dim(down_maps, adapter_index * rank, rank, 1)
        down_keep = lax.dynamic_slice_in_dim(down_map, tensor_part * half_width, half_width, 0)
        low_rank = dot(normed, down_map, 1, 0).astype(jnp.bfloat16)
        term_b = 2.0 * dot(low_rank, masked, 0, 0)
        marks = picker.astype(jnp.float32)[:, None, None]
        totals = lax.psum((marks * term_a[None], marks * term_b[None]), "dp")
        grad_a = lax.dynamic_index_in_dim(totals[0], tenant_slot, 0, keepdims=True)
        grad_b = lax.dynamic_index_in_dim(totals[1], tenant_slot, 0, keepdims=True)
        held, masks, last = middle_phases(row_parts(slots))
        got, plan = last_phase(held, masks, last)

    own, theirs, weight = forward(held + got, plan, normed, low_rank, mine, 0, cut)
    values = (own + swap_cores(theirs)).astype(jnp.bfloat16)
    part = jnp.reshape(tensor_part, (1,))
    values = last_values(part, gathered, normed, low_rank, mine, values)
    gradient = input_gradient(part, weight, gathered, mine, other, scaled_t, down_keep)
    return (values, gradient, grad_a, grad_b)


def solution(mesh):
    return jax.shard_map(
        shards,
        mesh=mesh,
        in_specs=(
            P(("groups", "dp"), None),
            P(("groups", "dp"), "tensor"),
            P("dp", "tensor"),
            P("dp", "groups"),
            P("groups", None, "tensor"),
            P("groups"),
            P("groups"),
            P("groups"),
        ),
        out_specs=(
            P(("groups", "dp"), "tensor"),
            P(("groups", "dp"), "tensor"),
            P(("groups", "dp"), None, "tensor"),
            P(("groups", "dp"), None, "tensor"),
        ),
        check_vma=False,
    )
```

time: 430 us -> 127 us (0.30)
  waiting for transfers between devices: 359 us -> 26.3 us
  starting transfers between devices: 0.2 us -> 38.9 us
  Pallas kernels: 0 us -> 35.7 us
  matrix products: 32.9 us -> 0 us
  other arithmetic: 12.8 us -> 5.12 us
  between operations: 21 us -> 15 us
    psum x2 -> x0, waiting for transfers between devices: 215 us -> none  [the longest x1 196 us: shards(): lax.psum((slot_mark[:, None, None] * term_a[None], slot_mark[:, None, Non...]
    all_gather x2 -> x1, waiting for transfers between devices: 143 us -> 0.01 us  [shards(): gathered = lax.all_gather(value_weight[:, cut:], ('dp', 'tensor'), axis=0)]
    ppermute x0 -> x29, starting transfers between devices: none -> 38.9 us  [the longest x22 31.8 us: exchange(): lax.ppermute(x, 'dp', [(i, i ^ mask) for i in range(lax.axis_size('dp'))])]
    pallas_call x0 -> x8, Pallas kernels: none -> 35.7 us  [the longest x4 17.9 us: kernel_call(): pl.pallas_call(kernel, out_shape=tuple(outs), in_specs=[SMEM] * len(scala...]
    dot_general x8 -> x0, matrix products: 32.9 us -> none  [the longest x3 15.5 us: contract_last(): lax.dot_general(left, right, (((1,), (1,)), ((), ())), preferred_element_...]
    ppermute x0 -> x29, waiting for transfers between devices: none -> 26.3 us  [the longest x22 25.4 us: exchange(): lax.ppermute(x, 'dp', [(i, i ^ mask) for i in range(lax.axis_size('dp'))])]
    reduce_sum x4 -> x0, other arithmetic: 6.45 us -> none  [the longest x1 1.94 us: shards(): valid_count = jnp.sum(picker * valid_tokens)]
  transfers between devices with their start and end apart: 5 -> 30, of which waited for: 4 -> 11; matrix products, arithmetic and copies ran while one was open for 8% -> 3% of each run, Pallas kernels for 0% -> 28%
where the time goes in v2:
time: 127 us; the launch traced here: 126 us
  starting transfers between devices  38.9 us (31%)
  Pallas kernels  35.7 us (28%)
  waiting for transfers between devices  26.3 us (21%)
  between operations  15 us (12%)
  other arithmetic  5.12 us (4%)
  local copies, waits for them, and re-layouts  5.11 us (4%)
    ppermute x22, starting transfers between devices, exchange(): lax.ppermute(x, 'dp', [(i, i ^ mask) for i in range(lax.axis_size('dp'))])  31.8 us
    ppermute x22, waiting for transfers between devices, exchange(): lax.ppermute(x, 'dp', [(i, i ^ mask) for i in range(lax.axis_size('dp'))])  25.4 us
    pallas_call x4, Pallas kernels, kernel_call(): pl.pallas_call(kernel, out_shape=tuple(outs), in_specs=[SMEM] * len(scala...  17.9 us
    pallas_call x1, Pallas kernels, input_gradient(): pl.pallas_call(gradient_kernel, grid_spec=pltpu.PrefetchScalarGridSpec(nu...  7.92 us
    pallas_call x1, Pallas kernels, last_values(): pl.pallas_call(last_values_kernel, grid_spec=pltpu.PrefetchScalarGridSpec...  6.09 us
    ppermute x4, starting transfers between devices, first_phase(): slots.append(lax.ppermute(piece, ('dp', 'tensor'), pairs))  5.78 us
    pallas_call x1, Pallas kernels, prepare(): pl.pallas_call(prepare_kernel, out_shape=(jax.ShapeDtypeStruct((row_count...  3.84 us
    unnamed x32, local copies, waits for them, and re-layouts  3.3 us
  transfers between devices with their start and end apart: 30, of which 11 were waited for; matrix products, arithmetic and copies ran while one was open for 3% of the time, Pallas kernels for 28%

profile of v2, /device:TPU:0, one launch (start us, length us, event | category | flops | bytes accessed | tf_op | source)
XLA Modules:
  0.0 126.1 jit_solution(4122275444928767284)
XLA Ops:
  7.2 1.7 %fusion.2 = (bf16[320,256]{1,0:T(8,128)(2,1)S(1)}, bf16[320,256]{1,0:T(8,128)(2,1)}) fusion(bf16[320,512]{1,0:T(8,128)(2,1)} %param.10), kind=kLoop, calls=%fused_computation.41 | loop fusion | bytes 655360 | tf_op jit(solution)/shard_map/slice | solution.py:559
  8.9 5.1 %collective-permute-start.11 = (bf16[320,256]{1,0:T(8,128)(2,1)S(1)}, bf16[320,256]{1,0:T(8,128)(2,1)S(1)}, u32[]{:S(2)}, u32[]{:S(2)}) collective-permute-start(bf16[320,256]{1,0:T(8,128)(2,1)S(1)} %get-tuple-element.52), channel_id=1, source_target_pairs={{9,0},{11,2},{13,4},{15,6},{25,1},{27,3},{29,5},{31,7},{1,8},{3,10... | collective-permute-start | bytes 491528 | tf_op jit(solution)/shard_map/ppermute | solution.py:132
  14.0 3.8 %shard_map.111 = (bf16[576,512]{1,0:T(8,128)(2,1)}, s32[1]{0:T(128)}, bf16[4,80,128]{2,1,0:T(8,128)(2,1)}, bf16[4,80,128]{2,1,0:T(8,128)(2,1)}, bf16[4,80,128]{2...) custom-call(s32[8]{0:T(128)} %devices_ref.1, s32[8]{0:T(128)} %adapter_ref.1, s32[8]{0:T(128)} %valid_ref.1, ...), custom_call_target="tpu_custom_call" | custom-call | flops 1 | bytes 1 | tf_op jit(solution)/shard_map/pallas_call | solution.py:368
  17.9 1.6 %collective-permute-start = (bf16[4,80,128]{2,1,0:T(8,128)(2,1)}, bf16[4,80,128]{2,1,0:T(8,128)(2,1)S(1)}, u32[]{:S(2)}, u32[]{:S(2)}) collective-permute-start(bf16[4,80,128]{2,1,0:T(8,128)(2,1)} %get-tuple-element.28), channel_id=1, source_target_pairs={{0,2},{2,0},{4,6},{6,4},{8,10},{10,8},{12,14},{14,12},{16,18},{18,... | collective-permute-start | bytes 245768 | tf_op jit(solution)/shard_map/ppermute | solution.py:39
  19.4 1.5 %collective-permute-start.1 = (bf16[4,80,128]{2,1,0:T(8,128)(2,1)}, bf16[4,80,128]{2,1,0:T(8,128)(2,1)S(1)}, u32[]{:S(2)}, u32[]{:S(2)}) collective-permute-start(bf16[4,80,128]{2,1,0:T(8,128)(2,1)} %get-tuple-element.29), channel_id=1, source_target_pairs={{0,4},{2,6},{4,0},{6,2},{8,12},{10,14},{12,8},{14,10},{16,20},{18,... | collective-permute-start | bytes 245768 | tf_op jit(solution)/shard_map/ppermute | solution.py:39
  21.4 1.6 %collective-permute-done.refs_1_ = bf16[4,80,128]{2,1,0:T(8,128)(2,1)S(1)} collective-permute-done((bf16[4,80,128]{2,1,0:T(8,128)(2,1)}, bf16[4,80,128]{2,1,0:T(8,128)(2,1)S(1)}, u32[]{:S(2)}, u32[]{:S(2)}) %collective-permute-start) | collective-permute-done | bytes 81952 | tf_op jit(solution)/shard_map/ppermute | solution.py:39
  24.9 2.8 %collective-permute-done.2.refs_3_ = bf16[4,80,128]{2,1,0:T(8,128)(2,1)S(1)} collective-permute-done((bf16[4,80,128]{2,1,0:T(8,128)(2,1)}, bf16[4,80,128]{2,1,0:T(8,128)(2,1)S(1)}, u32[]{:S(2)}, u32[]{:S(2)}) %collective-permute-start.2) | collective-permute-done | bytes 81952 | tf_op jit(solution)/shard_map/ppermute | solution.py:39
  28.3 1.8 %shard_map.112 = (bf16[4,80,128]{2,1,0:T(8,128)(2,1)}, bf16[4,80,128]{2,1,0:T(8,128)(2,1)}, bf16[4,80,128]{2,1,0:T(8,128)(2,1)}, bf16[4,80,128]{2,1,0:T(8,128)(2,1)}) custom-call(bf16[4,80,128]{2,1,0:T(8,128)(2,1)} %get-tuple-element.27.refs_0_, bf16[4,80,128]{2,1,0:T(8,128)(2,1)} %copy-done.11, bf16[4,80,128]{2,1,0:T(8,128)(2,1)} %copy-done.12, ...), custom_call_target="tpu_custom_call" | custom-call | flops 1 | bytes 1 | tf_op jit(solution)/shard_map/pallas_call | solution.py:93
  31.8 4.6 %collective-permute-start.5 = (bf16[4,80,128]{2,1,0:T(8,128)(2,1)}, bf16[4,80,128]{2,1,0:T(8,128)(2,1)S(1)}, u32[]{:S(2)}, u32[]{:S(2)}) collective-permute-start(bf16[4,80,128]{2,1,0:T(8,128)(2,1)} %get-tuple-element.34), channel_id=1, source_target_pairs={{0,24},{2,26},{4,28},{6,30},{8,16},{10,18},{12,20},{14,22},{16,8},... | collective-permute-start | bytes 245768 | tf_op jit(solution)/shard_map/ppermute | solution.py:39
  39.8 2.1 %collective-permute-done.4 = bf16[4,80,128]{2,1,0:T(8,128)(2,1)S(1)} collective-permute-done((bf16[4,80,128]{2,1,0:T(8,128)(2,1)}, bf16[4,80,128]{2,1,0:T(8,128)(2,1)S(1)}, u32[]{:S(2)}, u32[]{:S(2)}) %collective-permute-start.4) | collective-permute-done | bytes 81952 | tf_op jit(solution)/shard_map/ppermute | solution.py:39
  45.0 3.6 %shard_map.113 = (bf16[64,512]{1,0:T(8,128)(2,1)}, f32[64,2560]{1,0:T(8,128)}) custom-call(bf16[576,512]{1,0:T(8,128)(2,1)} %get-tuple-element.35.refs_0_.refs_3_.refs_1_.up_ref.mine_ref, bf16[576,512]{1,0:T(8,128)(2,1)} %copy-done.1, bf16[512,5120]{1,0:T(8,128)(2,1)} %normed_ref.1), custom_call_target="tpu_custom_call" | custom-call | flops 1 | bytes 1 | tf_op jit(solution)/shard_map/pallas_call | solution.py:93
  49.3 6.7 %shard_map.114 = (bf16[512,64]{1,0:T(8,128)(2,1)}, bf16[2560,64]{1,0:T(8,128)(2,1)}, f32[64,512]{1,0:T(8,128)}, f32[16,3072]{1,0:T(8,128)}, f32[16,3072]{1,0:T(8...) custom-call(s32[1]{0:T(128)} %get-tuple-element.26.refs_0_, bf16[4,4,80,128]{3,2,1,0:T(8,128)(2,1)} %copy-done.2, ...), custom_call_target="tpu_custom_call" | custom-call | flops 1 | bytes 1 | tf_op jit(solution)/shard_map/pallas_call | solution.py:93
  60.5 1.5 %collective-permute-start.15 = (bf16[8,160,256]{2,1,0:T(8,128)(2,1)S(1)}, bf16[8,160,256]{2,1,0:T(8,128)(2,1)S(1)}, u32[]{:S(2)}, u32[]{:S(2)}) collective-permute-start(bf16[8,160,256]{2,1,0:T(8,128)(2,1)S(1)} %constant_dynamic-update-slice_fusion.5.refs_3_), channel_id=1, source_target_pairs={{0,2},{2,0},{4,6},{6,4},{8,10},{10,8},{12,14},{14,12},{16,18},{18,... | collective-permute-start | bytes 1966088 | tf_op jit(solution)/shard_map/ppermute | solution.py:39
  62.0 2.1 %collective-permute-done.17 = f32[16,3072]{1,0:T(8,128)S(1)} collective-permute-done((f32[16,3072]{1,0:T(8,128)}, f32[16,3072]{1,0:T(8,128)S(1)}, u32[]{:S(2)}, u32[]{:S(2)}) %collective-permute-start.17) | collective-permute-done | bytes 196640 | tf_op jit(solution)/shard_map/ppermute | solution.py:39
  64.1 5.7 %collective-permute-done.18 = f32[16,3072]{1,0:T(8,128)S(1)} collective-permute-done((f32[16,3072]{1,0:T(8,128)}, f32[16,3072]{1,0:T(8,128)S(1)}, u32[]{:S(2)}, u32[]{:S(2)}) %collective-permute-start.18) | collective-permute-done | bytes 196640 | tf_op jit(solution)/shard_map/ppermute | solution.py:39
  70.7 2.9 %collective-permute-start.20 = (f32[16,768]{1,0:T(8,128)S(1)}, f32[16,768]{1,0:T(8,128)S(1)}, u32[]{:S(2)}, u32[]{:S(2)}) collective-permute-start(f32[16,768]{1,0:T(8,128)S(1)} %get-tuple-element.54), channel_id=1, source_target_pairs={{0,8},{2,10},{4,12},{6,14},{8,0},{10,2},{12,4},{14,6},{16,24},{18,... | collective-permute-start | bytes 147464 | tf_op jit(solution)/shard_map/ppermute | solution.py:39
  73.6 3.5 %collective-permute-start.22 = (f32[16,768]{1,0:T(8,128)S(1)}, f32[16,768]{1,0:T(8,128)S(1)}, u32[]{:S(2)}, u32[]{:S(2)}) collective-permute-start(f32[16,768]{1,0:T(8,128)S(1)} %get-tuple-element.55), channel_id=1, source_target_pairs={{0,24},{2,26},{4,28},{6,30},{8,16},{10,18},{12,20},{14,22},{16,8},... | collective-permute-start | bytes 147464 | tf_op jit(solution)/shard_map/ppermute | solution.py:39
  77.1 3.9 %collective-permute-done.22 = f32[16,768]{1,0:T(8,128)S(1)} collective-permute-done((f32[16,768]{1,0:T(8,128)S(1)}, f32[16,768]{1,0:T(8,128)S(1)}, u32[]{:S(2)}, u32[]{:S(2)}) %collective-permute-start.22) | collective-permute-done | bytes 49184 | tf_op jit(solution)/shard_map/ppermute | solution.py:39
  82.2 1.7 %collective-permute-start.24 = (bf16[16,768]{1,0:T(8,128)(2,1)S(1)}, bf16[16,768]{1,0:T(8,128)(2,1)S(1)}, u32[]{:S(2)}, u32[]{:S(2)}) collective-permute-start(bf16[16,768]{1,0:T(8,128)(2,1)S(1)} %add_convert_fusion.1), channel_id=1, source_target_pairs={{0,16},{2,18},{4,20},{6,22},{8,24},{10,26},{12,28},{14,30},{16,0},... | collective-permute-start | bytes 73736 | tf_op jit(solution)/shard_map/ppermute | solution.py:39
  83.9 2.7 %collective-permute-start.23 = (bf16[16,768]{1,0:T(8,128)(2,1)S(1)}, bf16[16,768]{1,0:T(8,128)(2,1)S(1)}, u32[]{:S(2)}, u32[]{:S(2)}) collective-permute-start(bf16[16,768]{1,0:T(8,128)(2,1)S(1)} %add_convert_fusion.1), channel_id=1, source_target_pairs={{0,24},{2,26},{4,28},{6,30},{8,16},{10,18},{12,20},{14,22},{16,8},... | collective-permute-start | bytes 73736 | tf_op jit(solution)/shard_map/ppermute | solution.py:39
  87.1 4.5 %collective-permute-done.14.refs_4_ = bf16[8,160,256]{2,1,0:T(8,128)(2,1)S(1)} collective-permute-done((bf16[8,160,256]{2,1,0:T(8,128)(2,1)S(1)}, bf16[8,160,256]{2,1,0:T(8,128)(2,1)S(1)}, u32[]{:S(2)}, u32[]{:S(2)}) %collective-permute-start.14) | collective-permute-done | bytes 655392 | tf_op jit(solution)/shard_map/ppermute | solution.py:39
  92.6 5.8 %shard_map.115 = (f32[512,256]{1,0:T(8,128)}, f32[512,256]{1,0:T(8,128)}, bf16[2,8,320,256]{3,2,1,0:T(8,128)(2,1)}) custom-call(bf16[512,64]{1,0:T(8,128)(2,1)} %get-tuple-element.37.refs_0_.low_ref, bf16[576,512]{1,0:T(8,128)(2,1)} %get-tuple-element.35.refs_0_.refs_3_.refs_1_.up_ref.mine_ref, bf16[8,160,256]{2,1,0:T(8,128)(2,1)} %copy-done.5, ...), custom_call_target="tpu_custom_call" | custom-call | flops 1 | bytes 1 | tf_op jit(solution)/shard_map/pallas_call | solution.py:93
  103.5 6.1 %shard_map.116 = bf16[512,512]{1,0:T(8,128)(2,1)} custom-call(s32[1]{0:T(128)} %bitcast.part_ref, bf16[16,2,320,256]{3,2,1,0:T(8,128)(2,1)} %bitcast.44, bf16[512,5120]{1,0:T(8,128)(2,1)} %normed_ref.1, bf16[512,64]{1,0:T(8,128)(2,1)} %get-tuple-element.37.refs_0_.low_ref, bf16[576,512]{1,0:T(8,128)(2,1)} %get-tuple-element.35.refs_0_.refs_3_.refs_1_.up_ref.mine_ref, ...), custom_call_target="tpu_custom_call" | custom-call | flops 1 | bytes 1 | tf_op jit(solution)/shard_map/pallas_call | solution.py:290
  109.6 7.9 %shard_map.117 = bf16[512,2560]{1,0:T(8,128)(2,1)} custom-call(s32[1]{0:T(128)} %bitcast.part_ref, bf16[2,8,320,256]{3,2,1,0:T(8,128)(2,1)} %get-tuple-element.40.weight_ref, bf16[16,2,320,256]{3,2,1,0:T(8,128)(2,1)} %bitcast.45, bf16[576,512]{1,0:T(8,128)(2,1)} %get-tuple-element.35.refs_0_.refs_3_.refs_1_.up_ref.mine_ref, bf16[576,512]{1,0:T(8,128)(2,1)} %copy-done.1, ...), custom_call_target="tpu_custom_call" | custom-call | flops 1 | bytes 1 | tf_op jit(solution)/shard_map/pallas_call | solution.py:242
  (97 shorter events, 26.2 us)
Async XLA Ops:
  7.2 92.1 %all-gather.3.cloned.1.call-start = ((), (), s32[]{:S(2)}) async-start(), calls=%async_computation | async-start | bytes 5406720 | tf_op jit(solution)/shard_map/all_gather | solution.py:560
  8.9 21.2 %collective-permute-start.11 = (bf16[320,256]{1,0:T(8,128)(2,1)S(1)}, bf16[320,256]{1,0:T(8,128)(2,1)S(1)}, u32[]{:S(2)}, u32[]{:S(2)}) collective-permute-start(bf16[320,256]{1,0:T(8,128)(2,1)S(1)} %get-tuple-element.52), channel_id=1, source_target_pairs={{9,0},{11,2},{13,4},{15,6},{25,1},{27,3},{29,5},{31,7},{1,8},{3,10... | collective-permute-start | bytes 491528 | tf_op jit(solution)/shard_map/ppermute | solution.py:132
  21.0 6.7 %collective-permute-start.2 = (bf16[4,80,128]{2,1,0:T(8,128)(2,1)}, bf16[4,80,128]{2,1,0:T(8,128)(2,1)S(1)}, u32[]{:S(2)}, u32[]{:S(2)}) collective-permute-start(bf16[4,80,128]{2,1,0:T(8,128)(2,1)} %get-tuple-element.30), channel_id=1, source_target_pairs={{0,6},{2,4},{4,2},{6,0},{8,14},{10,12},{12,10},{14,8},{16,22},{18,... | collective-permute-start | bytes 245768 | tf_op jit(solution)/shard_map/ppermute | solution.py:39
  21.4 8.8 %collective-permute-start.10 = (bf16[320,256]{1,0:T(8,128)(2,1)S(1)}, bf16[320,256]{1,0:T(8,128)(2,1)S(1)}, u32[]{:S(2)}, u32[]{:S(2)}) collective-permute-start(bf16[320,256]{1,0:T(8,128)(2,1)S(1)} %get-tuple-element.52), channel_id=1, source_target_pairs={{1,0},{3,2},{5,4},{7,6},{17,1},{19,3},{21,5},{23,7},{9,8},{11,10},... | collective-permute-start | bytes 491528 | tf_op jit(solution)/shard_map/ppermute | solution.py:132
  23.0 8.8 %collective-permute-start.9 = (bf16[320,256]{1,0:T(8,128)(2,1)S(1)}, bf16[320,256]{1,0:T(8,128)(2,1)S(1)}, u32[]{:S(2)}, u32[]{:S(2)}) collective-permute-start(bf16[320,256]{1,0:T(8,128)(2,1)S(1)} %get-tuple-element.52), channel_id=1, source_target_pairs={{8,0},{10,2},{12,4},{14,6},{24,1},{26,3},{28,5},{30,7},{0,8},{2,10... | collective-permute-start | bytes 491528 | tf_op jit(solution)/shard_map/ppermute | solution.py:132
  24.3 12.1 %collective-permute-start.8 = (bf16[320,256]{1,0:T(8,128)(2,1)S(1)}, bf16[320,256]{1,0:T(8,128)(2,1)S(1)}, u32[]{:S(2)}, u32[]{:S(2)}) collective-permute-start(bf16[320,256]{1,0:T(8,128)(2,1)S(1)} %get-tuple-element.52), channel_id=1, source_target_pairs={{0,0},{2,2},{4,4},{6,6},{16,1},{18,3},{20,5},{22,7},{8,8},{10,10},... | collective-permute-start | bytes 491528 | tf_op jit(solution)/shard_map/ppermute | solution.py:132
  27.7 16.5 %collective-permute-start.7 = (bf16[576,512]{1,0:T(8,128)(2,1)}, bf16[576,512]{1,0:T(8,128)(2,1)S(1)}, u32[]{:S(2)}, u32[]{:S(2)}) collective-permute-start(bf16[576,512]{1,0:T(8,128)(2,1)} %get-tuple-element.35.refs_0_.refs_3_.refs_1_.up_ref.mine_ref), channel_id=1, source_target_pairs={{0,1},{1,0},{2,3},{3,2},{4,5},{5,4},{6,7},{7,6},{8,9},{9,8},{10,11... | collective-permute-start | bytes 1769480 | tf_op jit(solution)/shard_map/ppermute | solution.py:35
  30.1 8.3 %collective-permute-start.3 = (bf16[4,80,128]{2,1,0:T(8,128)(2,1)}, bf16[4,80,128]{2,1,0:T(8,128)(2,1)S(1)}, u32[]{:S(2)}, u32[]{:S(2)}) collective-permute-start(bf16[4,80,128]{2,1,0:T(8,128)(2,1)} %get-tuple-element.32), channel_id=1, source_target_pairs={{0,8},{2,10},{4,12},{6,14},{8,0},{10,2},{12,4},{14,6},{16,24},{18,... | collective-permute-start | bytes 245768 | tf_op jit(solution)/shard_map/ppermute | solution.py:39
  30.3 11.7 %collective-permute-start.4 = (bf16[4,80,128]{2,1,0:T(8,128)(2,1)}, bf16[4,80,128]{2,1,0:T(8,128)(2,1)S(1)}, u32[]{:S(2)}, u32[]{:S(2)}) collective-permute-start(bf16[4,80,128]{2,1,0:T(8,128)(2,1)} %get-tuple-element.33), channel_id=1, source_target_pairs={{0,16},{2,18},{4,20},{6,22},{8,24},{10,26},{12,28},{14,30},{16,0},... | collective-permute-start | bytes 245768 | tf_op jit(solution)/shard_map/ppermute | solution.py:39
  31.8 10.1 %collective-permute-start.5 = (bf16[4,80,128]{2,1,0:T(8,128)(2,1)}, bf16[4,80,128]{2,1,0:T(8,128)(2,1)S(1)}, u32[]{:S(2)}, u32[]{:S(2)}) collective-permute-start(bf16[4,80,128]{2,1,0:T(8,128)(2,1)} %get-tuple-element.34), channel_id=1, source_target_pairs={{0,24},{2,26},{4,28},{6,30},{8,16},{10,18},{12,20},{14,22},{16,8},... | collective-permute-start | bytes 245768 | tf_op jit(solution)/shard_map/ppermute | solution.py:39
  36.5 23.1 %collective-permute-start.12 = (bf16[4,160,256]{2,1,0:T(8,128)(2,1)S(1)}, bf16[4,160,256]{2,1,0:T(8,128)(2,1)S(1)}, u32[]{:S(2)}, u32[]{:S(2)}) collective-permute-start(bf16[4,160,256]{2,1,0:T(8,128)(2,1)S(1)} %pad_maximum_fusion.1), channel_id=1, source_target_pairs={{0,2},{2,0},{4,6},{6,4},{8,10},{10,8},{12,14},{14,12},{16,18},{18,... | collective-permute-start | bytes 983048 | tf_op jit(solution)/shard_map/ppermute | solution.py:39
  38.5 22.0 %collective-permute-start.13 = (bf16[4,160,256]{2,1,0:T(8,128)(2,1)S(1)}, bf16[4,160,256]{2,1,0:T(8,128)(2,1)S(1)}, u32[]{:S(2)}, u32[]{:S(2)}) collective-permute-start(bf16[4,160,256]{2,1,0:T(8,128)(2,1)S(1)} %pad_maximum_fusion.2), channel_id=1, source_target_pairs={{0,4},{2,6},{4,0},{6,2},{8,12},{10,14},{12,8},{14,10},{16,20},{18,... | collective-permute-start | bytes 983048 | tf_op jit(solution)/shard_map/ppermute | solution.py:39
  56.0 8.0 %collective-permute-start.17 = (f32[16,3072]{1,0:T(8,128)}, f32[16,3072]{1,0:T(8,128)S(1)}, u32[]{:S(2)}, u32[]{:S(2)}) collective-permute-start(f32[16,3072]{1,0:T(8,128)} %get-tuple-element.44), channel_id=1, source_target_pairs={{0,2},{2,0},{4,6},{6,4},{8,10},{10,8},{12,14},{14,12},{16,18},{18,... | collective-permute-start | bytes 589832 | tf_op jit(solution)/shard_map/ppermute | solution.py:39
  56.8 12.9 %collective-permute-start.18 = (f32[16,3072]{1,0:T(8,128)}, f32[16,3072]{1,0:T(8,128)S(1)}, u32[]{:S(2)}, u32[]{:S(2)}) collective-permute-start(f32[16,3072]{1,0:T(8,128)} %get-tuple-element.45), channel_id=1, source_target_pairs={{0,4},{2,6},{4,0},{6,2},{8,12},{10,14},{12,8},{14,10},{16,20},{18,... | collective-permute-start | bytes 589832 | tf_op jit(solution)/shard_map/ppermute | solution.py:39
  58.3 11.4 %collective-permute-start.19 = (f32[16,3072]{1,0:T(8,128)}, f32[16,3072]{1,0:T(8,128)S(1)}, u32[]{:S(2)}, u32[]{:S(2)}) collective-permute-start(f32[16,3072]{1,0:T(8,128)} %get-tuple-element.46), channel_id=1, source_target_pairs={{0,6},{2,4},{4,2},{6,0},{8,14},{10,12},{12,10},{14,8},{16,22},{18,... | collective-permute-start | bytes 589832 | tf_op jit(solution)/shard_map/ppermute | solution.py:39
  59.6 31.9 %collective-permute-start.14 = (bf16[8,160,256]{2,1,0:T(8,128)(2,1)S(1)}, bf16[8,160,256]{2,1,0:T(8,128)(2,1)S(1)}, u32[]{:S(2)}, u32[]{:S(2)}) collective-permute-start(bf16[8,160,256]{2,1,0:T(8,128)(2,1)S(1)} %constant_dynamic-update-slice_fusion.refs_2_), channel_id=1, source_target_pairs={{0,4},{2,6},{4,0},{6,2},{8,12},{10,14},{12,8},{14,10},{16,20},{18,... | collective-permute-start | bytes 1966088 | tf_op jit(solution)/shard_map/ppermute | solution.py:39
  60.5 31.1 %collective-permute-start.15 = (bf16[8,160,256]{2,1,0:T(8,128)(2,1)S(1)}, bf16[8,160,256]{2,1,0:T(8,128)(2,1)S(1)}, u32[]{:S(2)}, u32[]{:S(2)}) collective-permute-start(bf16[8,160,256]{2,1,0:T(8,128)(2,1)S(1)} %constant_dynamic-update-slice_fusion.5.refs_3_), channel_id=1, source_target_pairs={{0,2},{2,0},{4,6},{6,4},{8,10},{10,8},{12,14},{14,12},{16,18},{18,... | collective-permute-start | bytes 1966088 | tf_op jit(solution)/shard_map/ppermute | solution.py:39
  73.6 7.4 %collective-permute-start.22 = (f32[16,768]{1,0:T(8,128)S(1)}, f32[16,768]{1,0:T(8,128)S(1)}, u32[]{:S(2)}, u32[]{:S(2)}) collective-permute-start(f32[16,768]{1,0:T(8,128)S(1)} %get-tuple-element.55), channel_id=1, source_target_pairs={{0,24},{2,26},{4,28},{6,30},{8,16},{10,18},{12,20},{14,22},{16,8},... | collective-permute-start | bytes 147464 | tf_op jit(solution)/shard_map/ppermute | solution.py:39
  82.1 16.5 %collective-permute-start.25 = (bf16[16,768]{1,0:T(8,128)(2,1)S(1)}, bf16[16,768]{1,0:T(8,128)(2,1)S(1)}, u32[]{:S(2)}, u32[]{:S(2)}) collective-permute-start(bf16[16,768]{1,0:T(8,128)(2,1)S(1)} %add_convert_fusion.1), channel_id=1, source_target_pairs={{0,8},{2,10},{4,12},{6,14},{8,0},{10,2},{12,4},{14,6},{16,24},{18,... | collective-permute-start | bytes 73736 | tf_op jit(solution)/shard_map/ppermute | solution.py:39
  82.2 16.4 %collective-permute-start.24 = (bf16[16,768]{1,0:T(8,128)(2,1)S(1)}, bf16[16,768]{1,0:T(8,128)(2,1)S(1)}, u32[]{:S(2)}, u32[]{:S(2)}) collective-permute-start(bf16[16,768]{1,0:T(8,128)(2,1)S(1)} %add_convert_fusion.1), channel_id=1, source_target_pairs={{0,16},{2,18},{4,20},{6,22},{8,24},{10,26},{12,28},{14,30},{16,0},... | collective-permute-start | bytes 73736 | tf_op jit(solution)/shard_map/ppermute | solution.py:39
  83.9 14.7 %collective-permute-start.23 = (bf16[16,768]{1,0:T(8,128)(2,1)S(1)}, bf16[16,768]{1,0:T(8,128)(2,1)S(1)}, u32[]{:S(2)}, u32[]{:S(2)}) collective-permute-start(bf16[16,768]{1,0:T(8,128)(2,1)S(1)} %add_convert_fusion.1), channel_id=1, source_target_pairs={{0,24},{2,26},{4,28},{6,30},{8,16},{10,18},{12,20},{14,22},{16,8},... | collective-permute-start | bytes 73736 | tf_op jit(solution)/shard_map/ppermute | solution.py:39
  99.3 18.3 %collective-permute-start.28 = (bf16[16,3072]{1,0:T(8,128)(2,1)}, bf16[16,3072]{1,0:T(8,128)(2,1)S(1)}, u32[]{:S(2)}, u32[]{:S(2)}) collective-permute-start(bf16[16,3072]{1,0:T(8,128)(2,1)} %shard_map.118), channel_id=1, source_target_pairs={{0,2},{2,0},{4,6},{6,4},{8,10},{10,8},{12,14},{14,12},{16,18},{18,... | collective-permute-start | bytes 294920 | tf_op jit(solution)/shard_map/ppermute | solution.py:39
  100.2 17.4 %collective-permute-start.27 = (bf16[16,3072]{1,0:T(8,128)(2,1)}, bf16[16,3072]{1,0:T(8,128)(2,1)S(1)}, u32[]{:S(2)}, u32[]{:S(2)}) collective-permute-start(bf16[16,3072]{1,0:T(8,128)(2,1)} %shard_map.118), channel_id=1, source_target_pairs={{0,4},{2,6},{4,0},{6,2},{8,12},{10,14},{12,8},{14,10},{16,20},{18,... | collective-permute-start | bytes 294920 | tf_op jit(solution)/shard_map/ppermute | solution.py:39
  101.3 16.2 %collective-permute-start.26 = (bf16[16,3072]{1,0:T(8,128)(2,1)}, bf16[16,3072]{1,0:T(8,128)(2,1)S(1)}, u32[]{:S(2)}, u32[]{:S(2)}) collective-permute-start(bf16[16,3072]{1,0:T(8,128)(2,1)} %shard_map.118), channel_id=1, source_target_pairs={{0,6},{2,4},{4,2},{6,0},{8,14},{10,12},{12,10},{14,8},{16,22},{18,... | collective-permute-start | bytes 294920 | tf_op jit(solution)/shard_map/ppermute | solution.py:39
  (20 other events, 141.4 us)
Sparse Core Ops, SparseCore 0:
  10.9 86.9 all-gather.2

commit v3 on v2

--- a/solution.py
+++ b/solution.py
@@ -236,7 +236,7 @@
     _, half, rows, cut = weight.shape
     columns = gathered.shape[3]
     rank, row_count = scaled_t.shape
-    blocks = tile_blocks(rows, half)
+    blocks = 2 * tile_blocks(rows, half)
     width, steps = blocks * rows, half // blocks
     masked = pl.BlockSpec((row_count, mine.shape[1]), lambda i, part: (0, 0))
     return pl.pallas_call(
@@ -281,7 +281,7 @@
 def last_values(part, gathered, normed, low_rank, mine, first):
     count, _, rows, columns = gathered.shape
     row_count = normed.shape[0]
-    blocks = 2 * tile_blocks(rows, count // 2)
+    blocks = 4 * tile_blocks(rows, count // 2)
     width = blocks * rows
 
     def whole(x):

time: 127 us -> 125 us (0.984)
  Pallas kernels: 35.7 us -> 34.2 us
  transfers between devices with their start and end apart: 30 -> 30, of which waited for: 11 -> 11; matrix products, arithmetic and copies ran while one was open for 3% -> 3% of each run, Pallas kernels for 28% -> 27%
where the time goes in v3:
time: 125 us
  starting transfers between devices  38.9 us (31%)
  Pallas kernels  34.2 us (27%)
  waiting for transfers between devices  26.3 us (21%)
  between operations  15 us (12%)
  other arithmetic  5.12 us (4%)
  local copies, waits for them, and re-layouts  5.11 us (4%)
    ppermute x22, starting transfers between devices, exchange(): lax.ppermute(x, 'dp', [(i, i ^ mask) for i in range(lax.axis_size('dp'))])  31.8 us
    ppermute x22, waiting for transfers between devices, exchange(): lax.ppermute(x, 'dp', [(i, i ^ mask) for i in range(lax.axis_size('dp'))])  25.4 us
    pallas_call x4, Pallas kernels, kernel_call(): pl.pallas_call(kernel, out_shape=tuple(outs), in_specs=[SMEM] * len(scala...  17.9 us
    pallas_call x1, Pallas kernels, input_gradient(): pl.pallas_call(gradient_kernel, grid_spec=pltpu.PrefetchScalarGridSpec(nu...  7.2 us
    ppermute x4, starting transfers between devices, first_phase(): slots.append(lax.ppermute(piece, ('dp', 'tensor'), pairs))  5.78 us
    pallas_call x1, Pallas kernels, last_values(): pl.pallas_call(last_values_kernel, grid_spec=pltpu.PrefetchScalarGridSpec...  5.27 us
    pallas_call x1, Pallas kernels, prepare(): pl.pallas_call(prepare_kernel, out_shape=(jax.ShapeDtypeStruct((row_count...  3.84 us
    unnamed x32, local copies, waits for them, and re-layouts  3.3 us
  transfers between devices with their start and end apart: 30, of which 11 were waited for; matrix products, arithmetic and copies ran while one was open for 3% of the time, Pallas kernels for 27%

profile of v3, /device:TPU:0, one launch (start us, length us, event | category | flops | bytes accessed | tf_op | source)
XLA Modules:
  0.0 124.6 jit_solution(16109348620711946803)
XLA Ops:
  7.2 1.7 %fusion.2 = (bf16[320,256]{1,0:T(8,128)(2,1)S(1)}, bf16[320,256]{1,0:T(8,128)(2,1)}) fusion(bf16[320,512]{1,0:T(8,128)(2,1)} %param.10), kind=kLoop, calls=%fused_computation.41 | loop fusion | bytes 655360 | tf_op jit(solution)/shard_map/slice | solution.py:559
  8.9 5.1 %collective-permute-start.11 = (bf16[320,256]{1,0:T(8,128)(2,1)S(1)}, bf16[320,256]{1,0:T(8,128)(2,1)S(1)}, u32[]{:S(2)}, u32[]{:S(2)}) collective-permute-start(bf16[320,256]{1,0:T(8,128)(2,1)S(1)} %get-tuple-element.52), channel_id=1, source_target_pairs={{9,0},{11,2},{13,4},{15,6},{25,1},{27,3},{29,5},{31,7},{1,8},{3,10... | collective-permute-start | bytes 491528 | tf_op jit(solution)/shard_map/ppermute | solution.py:132
  14.0 3.8 %shard_map.111 = (bf16[576,512]{1,0:T(8,128)(2,1)}, s32[1]{0:T(128)}, bf16[4,80,128]{2,1,0:T(8,128)(2,1)}, bf16[4,80,128]{2,1,0:T(8,128)(2,1)}, bf16[4,80,128]{2...) custom-call(s32[8]{0:T(128)} %devices_ref.1, s32[8]{0:T(128)} %adapter_ref.1, s32[8]{0:T(128)} %valid_ref.1, ...), custom_call_target="tpu_custom_call" | custom-call | flops 1 | bytes 1 | tf_op jit(solution)/shard_map/pallas_call | solution.py:368
  17.9 1.6 %collective-permute-start = (bf16[4,80,128]{2,1,0:T(8,128)(2,1)}, bf16[4,80,128]{2,1,0:T(8,128)(2,1)S(1)}, u32[]{:S(2)}, u32[]{:S(2)}) collective-permute-start(bf16[4,80,128]{2,1,0:T(8,128)(2,1)} %get-tuple-element.28), channel_id=1, source_target_pairs={{0,2},{2,0},{4,6},{6,4},{8,10},{10,8},{12,14},{14,12},{16,18},{18,... | collective-permute-start | bytes 245768 | tf_op jit(solution)/shard_map/ppermute | solution.py:39
  19.4 1.5 %collective-permute-start.1 = (bf16[4,80,128]{2,1,0:T(8,128)(2,1)}, bf16[4,80,128]{2,1,0:T(8,128)(2,1)S(1)}, u32[]{:S(2)}, u32[]{:S(2)}) collective-permute-start(bf16[4,80,128]{2,1,0:T(8,128)(2,1)} %get-tuple-element.29), channel_id=1, source_target_pairs={{0,4},{2,6},{4,0},{6,2},{8,12},{10,14},{12,8},{14,10},{16,20},{18,... | collective-permute-start | bytes 245768 | tf_op jit(solution)/shard_map/ppermute | solution.py:39
  21.4 1.6 %collective-permute-done.refs_1_ = bf16[4,80,128]{2,1,0:T(8,128)(2,1)S(1)} collective-permute-done((bf16[4,80,128]{2,1,0:T(8,128)(2,1)}, bf16[4,80,128]{2,1,0:T(8,128)(2,1)S(1)}, u32[]{:S(2)}, u32[]{:S(2)}) %collective-permute-start) | collective-permute-done | bytes 81952 | tf_op jit(solution)/shard_map/ppermute | solution.py:39
  24.9 2.8 %collective-permute-done.2.refs_3_ = bf16[4,80,128]{2,1,0:T(8,128)(2,1)S(1)} collective-permute-done((bf16[4,80,128]{2,1,0:T(8,128)(2,1)}, bf16[4,80,128]{2,1,0:T(8,128)(2,1)S(1)}, u32[]{:S(2)}, u32[]{:S(2)}) %collective-permute-start.2) | collective-permute-done | bytes 81952 | tf_op jit(solution)/shard_map/ppermute | solution.py:39
  28.3 1.8 %shard_map.112 = (bf16[4,80,128]{2,1,0:T(8,128)(2,1)}, bf16[4,80,128]{2,1,0:T(8,128)(2,1)}, bf16[4,80,128]{2,1,0:T(8,128)(2,1)}, bf16[4,80,128]{2,1,0:T(8,128)(2,1)}) custom-call(bf16[4,80,128]{2,1,0:T(8,128)(2,1)} %get-tuple-element.27.refs_0_, bf16[4,80,128]{2,1,0:T(8,128)(2,1)} %copy-done.11, bf16[4,80,128]{2,1,0:T(8,128)(2,1)} %copy-done.12, ...), custom_call_target="tpu_custom_call" | custom-call | flops 1 | bytes 1 | tf_op jit(solution)/shard_map/pallas_call | solution.py:93
  31.8 4.6 %collective-permute-start.5 = (bf16[4,80,128]{2,1,0:T(8,128)(2,1)}, bf16[4,80,128]{2,1,0:T(8,128)(2,1)S(1)}, u32[]{:S(2)}, u32[]{:S(2)}) collective-permute-start(bf16[4,80,128]{2,1,0:T(8,128)(2,1)} %get-tuple-element.34), channel_id=1, source_target_pairs={{0,24},{2,26},{4,28},{6,30},{8,16},{10,18},{12,20},{14,22},{16,8},... | collective-permute-start | bytes 245768 | tf_op jit(solution)/shard_map/ppermute | solution.py:39
  39.8 2.1 %collective-permute-done.4 = bf16[4,80,128]{2,1,0:T(8,128)(2,1)S(1)} collective-permute-done((bf16[4,80,128]{2,1,0:T(8,128)(2,1)}, bf16[4,80,128]{2,1,0:T(8,128)(2,1)S(1)}, u32[]{:S(2)}, u32[]{:S(2)}) %collective-permute-start.4) | collective-permute-done | bytes 81952 | tf_op jit(solution)/shard_map/ppermute | solution.py:39
  45.0 3.6 %shard_map.113 = (bf16[64,512]{1,0:T(8,128)(2,1)}, f32[64,2560]{1,0:T(8,128)}) custom-call(bf16[576,512]{1,0:T(8,128)(2,1)} %get-tuple-element.35.refs_0_.refs_3_.refs_1_.up_ref.mine_ref, bf16[576,512]{1,0:T(8,128)(2,1)} %copy-done.1, bf16[512,5120]{1,0:T(8,128)(2,1)} %normed_ref.1), custom_call_target="tpu_custom_call" | custom-call | flops 1 | bytes 1 | tf_op jit(solution)/shard_map/pallas_call | solution.py:93
  49.3 6.7 %shard_map.114 = (bf16[512,64]{1,0:T(8,128)(2,1)}, bf16[2560,64]{1,0:T(8,128)(2,1)}, f32[64,512]{1,0:T(8,128)}, f32[16,3072]{1,0:T(8,128)}, f32[16,3072]{1,0:T(8...) custom-call(s32[1]{0:T(128)} %get-tuple-element.26.refs_0_, bf16[4,4,80,128]{3,2,1,0:T(8,128)(2,1)} %copy-done.2, ...), custom_call_target="tpu_custom_call" | custom-call | flops 1 | bytes 1 | tf_op jit(solution)/shard_map/pallas_call | solution.py:93
  60.5 1.5 %collective-permute-start.15 = (bf16[8,160,256]{2,1,0:T(8,128)(2,1)S(1)}, bf16[8,160,256]{2,1,0:T(8,128)(2,1)S(1)}, u32[]{:S(2)}, u32[]{:S(2)}) collective-permute-start(bf16[8,160,256]{2,1,0:T(8,128)(2,1)S(1)} %constant_dynamic-update-slice_fusion.5.refs_3_), channel_id=1, source_target_pairs={{0,2},{2,0},{4,6},{6,4},{8,10},{10,8},{12,14},{14,12},{16,18},{18,... | collective-permute-start | bytes 1966088 | tf_op jit(solution)/shard_map/ppermute | solution.py:39
  62.0 2.1 %collective-permute-done.17 = f32[16,3072]{1,0:T(8,128)S(1)} collective-permute-done((f32[16,3072]{1,0:T(8,128)}, f32[16,3072]{1,0:T(8,128)S(1)}, u32[]{:S(2)}, u32[]{:S(2)}) %collective-permute-start.17) | collective-permute-done | bytes 196640 | tf_op jit(solution)/shard_map/ppermute | solution.py:39
  64.1 5.7 %collective-permute-done.18 = f32[16,3072]{1,0:T(8,128)S(1)} collective-permute-done((f32[16,3072]{1,0:T(8,128)}, f32[16,3072]{1,0:T(8,128)S(1)}, u32[]{:S(2)}, u32[]{:S(2)}) %collective-permute-start.18) | collective-permute-done | bytes 196640 | tf_op jit(solution)/shard_map/ppermute | solution.py:39
  70.7 2.9 %collective-permute-start.20 = (f32[16,768]{1,0:T(8,128)S(1)}, f32[16,768]{1,0:T(8,128)S(1)}, u32[]{:S(2)}, u32[]{:S(2)}) collective-permute-start(f32[16,768]{1,0:T(8,128)S(1)} %get-tuple-element.54), channel_id=1, source_target_pairs={{0,8},{2,10},{4,12},{6,14},{8,0},{10,2},{12,4},{14,6},{16,24},{18,... | collective-permute-start | bytes 147464 | tf_op jit(solution)/shard_map/ppermute | solution.py:39
  73.6 3.5 %collective-permute-start.22 = (f32[16,768]{1,0:T(8,128)S(1)}, f32[16,768]{1,0:T(8,128)S(1)}, u32[]{:S(2)}, u32[]{:S(2)}) collective-permute-start(f32[16,768]{1,0:T(8,128)S(1)} %get-tuple-element.55), channel_id=1, source_target_pairs={{0,24},{2,26},{4,28},{6,30},{8,16},{10,18},{12,20},{14,22},{16,8},... | collective-permute-start | bytes 147464 | tf_op jit(solution)/shard_map/ppermute | solution.py:39
  77.1 3.9 %collective-permute-done.22 = f32[16,768]{1,0:T(8,128)S(1)} collective-permute-done((f32[16,768]{1,0:T(8,128)S(1)}, f32[16,768]{1,0:T(8,128)S(1)}, u32[]{:S(2)}, u32[]{:S(2)}) %collective-permute-start.22) | collective-permute-done | bytes 49184 | tf_op jit(solution)/shard_map/ppermute | solution.py:39
  82.2 1.7 %collective-permute-start.24 = (bf16[16,768]{1,0:T(8,128)(2,1)S(1)}, bf16[16,768]{1,0:T(8,128)(2,1)S(1)}, u32[]{:S(2)}, u32[]{:S(2)}) collective-permute-start(bf16[16,768]{1,0:T(8,128)(2,1)S(1)} %add_convert_fusion.1), channel_id=1, source_target_pairs={{0,16},{2,18},{4,20},{6,22},{8,24},{10,26},{12,28},{14,30},{16,0},... | collective-permute-start | bytes 73736 | tf_op jit(solution)/shard_map/ppermute | solution.py:39
  83.9 2.7 %collective-permute-start.23 = (bf16[16,768]{1,0:T(8,128)(2,1)S(1)}, bf16[16,768]{1,0:T(8,128)(2,1)S(1)}, u32[]{:S(2)}, u32[]{:S(2)}) collective-permute-start(bf16[16,768]{1,0:T(8,128)(2,1)S(1)} %add_convert_fusion.1), channel_id=1, source_target_pairs={{0,24},{2,26},{4,28},{6,30},{8,16},{10,18},{12,20},{14,22},{16,8},... | collective-permute-start | bytes 73736 | tf_op jit(solution)/shard_map/ppermute | solution.py:39
  87.1 4.5 %collective-permute-done.14.refs_4_ = bf16[8,160,256]{2,1,0:T(8,128)(2,1)S(1)} collective-permute-done((bf16[8,160,256]{2,1,0:T(8,128)(2,1)S(1)}, bf16[8,160,256]{2,1,0:T(8,128)(2,1)S(1)}, u32[]{:S(2)}, u32[]{:S(2)}) %collective-permute-start.14) | collective-permute-done | bytes 655392 | tf_op jit(solution)/shard_map/ppermute | solution.py:39
  92.6 5.8 %shard_map.115 = (f32[512,256]{1,0:T(8,128)}, f32[512,256]{1,0:T(8,128)}, bf16[2,8,320,256]{3,2,1,0:T(8,128)(2,1)}) custom-call(bf16[512,64]{1,0:T(8,128)(2,1)} %get-tuple-element.37.refs_0_.low_ref, bf16[576,512]{1,0:T(8,128)(2,1)} %get-tuple-element.35.refs_0_.refs_3_.refs_1_.up_ref.mine_ref, bf16[8,160,256]{2,1,0:T(8,128)(2,1)} %copy-done.5, ...), custom_call_target="tpu_custom_call" | custom-call | flops 1 | bytes 1 | tf_op jit(solution)/shard_map/pallas_call | solution.py:93
  103.5 5.3 %shard_map.116 = bf16[512,512]{1,0:T(8,128)(2,1)} custom-call(s32[1]{0:T(128)} %bitcast.part_ref, bf16[16,2,320,256]{3,2,1,0:T(8,128)(2,1)} %bitcast.44, bf16[512,5120]{1,0:T(8,128)(2,1)} %normed_ref.1, bf16[512,64]{1,0:T(8,128)(2,1)} %get-tuple-element.37.refs_0_.low_ref, bf16[576,512]{1,0:T(8,128)(2,1)} %get-tuple-element.35.refs_0_.refs_3_.refs_1_.up_ref.mine_ref, ...), custom_call_target="tpu_custom_call" | custom-call | flops 1 | bytes 1 | tf_op jit(solution)/shard_map/pallas_call | solution.py:290
  108.8 7.2 %shard_map.117 = bf16[512,2560]{1,0:T(8,128)(2,1)} custom-call(s32[1]{0:T(128)} %bitcast.part_ref, bf16[2,8,320,256]{3,2,1,0:T(8,128)(2,1)} %get-tuple-element.40.weight_ref, bf16[16,2,320,256]{3,2,1,0:T(8,128)(2,1)} %bitcast.45, bf16[576,512]{1,0:T(8,128)(2,1)} %get-tuple-element.35.refs_0_.refs_3_.refs_1_.up_ref.mine_ref, bf16[576,512]{1,0:T(8,128)(2,1)} %copy-done.1, ...), custom_call_target="tpu_custom_call" | custom-call | flops 1 | bytes 1 | tf_op jit(solution)/shard_map/pallas_call | solution.py:242
  (97 shorter events, 26.2 us)
Async XLA Ops:
  7.2 92.1 %all-gather.3.cloned.1.call-start = ((), (), s32[]{:S(2)}) async-start(), calls=%async_computation | async-start | bytes 5406720 | tf_op jit(solution)/shard_map/all_gather | solution.py:560
  8.9 21.2 %collective-permute-start.11 = (bf16[320,256]{1,0:T(8,128)(2,1)S(1)}, bf16[320,256]{1,0:T(8,128)(2,1)S(1)}, u32[]{:S(2)}, u32[]{:S(2)}) collective-permute-start(bf16[320,256]{1,0:T(8,128)(2,1)S(1)} %get-tuple-element.52), channel_id=1, source_target_pairs={{9,0},{11,2},{13,4},{15,6},{25,1},{27,3},{29,5},{31,7},{1,8},{3,10... | collective-permute-start | bytes 491528 | tf_op jit(solution)/shard_map/ppermute | solution.py:132
  21.0 6.7 %collective-permute-start.2 = (bf16[4,80,128]{2,1,0:T(8,128)(2,1)}, bf16[4,80,128]{2,1,0:T(8,128)(2,1)S(1)}, u32[]{:S(2)}, u32[]{:S(2)}) collective-permute-start(bf16[4,80,128]{2,1,0:T(8,128)(2,1)} %get-tuple-element.30), channel_id=1, source_target_pairs={{0,6},{2,4},{4,2},{6,0},{8,14},{10,12},{12,10},{14,8},{16,22},{18,... | collective-permute-start | bytes 245768 | tf_op jit(solution)/shard_map/ppermute | solution.py:39
  21.4 8.8 %collective-permute-start.10 = (bf16[320,256]{1,0:T(8,128)(2,1)S(1)}, bf16[320,256]{1,0:T(8,128)(2,1)S(1)}, u32[]{:S(2)}, u32[]{:S(2)}) collective-permute-start(bf16[320,256]{1,0:T(8,128)(2,1)S(1)} %get-tuple-element.52), channel_id=1, source_target_pairs={{1,0},{3,2},{5,4},{7,6},{17,1},{19,3},{21,5},{23,7},{9,8},{11,10},... | collective-permute-start | bytes 491528 | tf_op jit(solution)/shard_map/ppermute | solution.py:132
  23.0 8.8 %collective-permute-start.9 = (bf16[320,256]{1,0:T(8,128)(2,1)S(1)}, bf16[320,256]{1,0:T(8,128)(2,1)S(1)}, u32[]{:S(2)}, u32[]{:S(2)}) collective-permute-start(bf16[320,256]{1,0:T(8,128)(2,1)S(1)} %get-tuple-element.52), channel_id=1, source_target_pairs={{8,0},{10,2},{12,4},{14,6},{24,1},{26,3},{28,5},{30,7},{0,8},{2,10... | collective-permute-start | bytes 491528 | tf_op jit(solution)/shard_map/ppermute | solution.py:132
  24.3 12.1 %collective-permute-start.8 = (bf16[320,256]{1,0:T(8,128)(2,1)S(1)}, bf16[320,256]{1,0:T(8,128)(2,1)S(1)}, u32[]{:S(2)}, u32[]{:S(2)}) collective-permute-start(bf16[320,256]{1,0:T(8,128)(2,1)S(1)} %get-tuple-element.52), channel_id=1, source_target_pairs={{0,0},{2,2},{4,4},{6,6},{16,1},{18,3},{20,5},{22,7},{8,8},{10,10},... | collective-permute-start | bytes 491528 | tf_op jit(solution)/shard_map/ppermute | solution.py:132
  27.7 16.5 %collective-permute-start.7 = (bf16[576,512]{1,0:T(8,128)(2,1)}, bf16[576,512]{1,0:T(8,128)(2,1)S(1)}, u32[]{:S(2)}, u32[]{:S(2)}) collective-permute-start(bf16[576,512]{1,0:T(8,128)(2,1)} %get-tuple-element.35.refs_0_.refs_3_.refs_1_.up_ref.mine_ref), channel_id=1, source_target_pairs={{0,1},{1,0},{2,3},{3,2},{4,5},{5,4},{6,7},{7,6},{8,9},{9,8},{10,11... | collective-permute-start | bytes 1769480 | tf_op jit(solution)/shard_map/ppermute | solution.py:35
  30.1 8.3 %collective-permute-start.3 = (bf16[4,80,128]{2,1,0:T(8,128)(2,1)}, bf16[4,80,128]{2,1,0:T(8,128)(2,1)S(1)}, u32[]{:S(2)}, u32[]{:S(2)}) collective-permute-start(bf16[4,80,128]{2,1,0:T(8,128)(2,1)} %get-tuple-element.32), channel_id=1, source_target_pairs={{0,8},{2,10},{4,12},{6,14},{8,0},{10,2},{12,4},{14,6},{16,24},{18,... | collective-permute-start | bytes 245768 | tf_op jit(solution)/shard_map/ppermute | solution.py:39
  30.3 11.7 %collective-permute-start.4 = (bf16[4,80,128]{2,1,0:T(8,128)(2,1)}, bf16[4,80,128]{2,1,0:T(8,128)(2,1)S(1)}, u32[]{:S(2)}, u32[]{:S(2)}) collective-permute-start(bf16[4,80,128]{2,1,0:T(8,128)(2,1)} %get-tuple-element.33), channel_id=1, source_target_pairs={{0,16},{2,18},{4,20},{6,22},{8,24},{10,26},{12,28},{14,30},{16,0},... | collective-permute-start | bytes 245768 | tf_op jit(solution)/shard_map/ppermute | solution.py:39
  31.8 10.1 %collective-permute-start.5 = (bf16[4,80,128]{2,1,0:T(8,128)(2,1)}, bf16[4,80,128]{2,1,0:T(8,128)(2,1)S(1)}, u32[]{:S(2)}, u32[]{:S(2)}) collective-permute-start(bf16[4,80,128]{2,1,0:T(8,128)(2,1)} %get-tuple-element.34), channel_id=1, source_target_pairs={{0,24},{2,26},{4,28},{6,30},{8,16},{10,18},{12,20},{14,22},{16,8},... | collective-permute-start | bytes 245768 | tf_op jit(solution)/shard_map/ppermute | solution.py:39
  36.5 23.1 %collective-permute-start.12 = (bf16[4,160,256]{2,1,0:T(8,128)(2,1)S(1)}, bf16[4,160,256]{2,1,0:T(8,128)(2,1)S(1)}, u32[]{:S(2)}, u32[]{:S(2)}) collective-permute-start(bf16[4,160,256]{2,1,0:T(8,128)(2,1)S(1)} %pad_maximum_fusion.1), channel_id=1, source_target_pairs={{0,2},{2,0},{4,6},{6,4},{8,10},{10,8},{12,14},{14,12},{16,18},{18,... | collective-permute-start | bytes 983048 | tf_op jit(solution)/shard_map/ppermute | solution.py:39
  38.5 22.0 %collective-permute-start.13 = (bf16[4,160,256]{2,1,0:T(8,128)(2,1)S(1)}, bf16[4,160,256]{2,1,0:T(8,128)(2,1)S(1)}, u32[]{:S(2)}, u32[]{:S(2)}) collective-permute-start(bf16[4,160,256]{2,1,0:T(8,128)(2,1)S(1)} %pad_maximum_fusion.2), channel_id=1, source_target_pairs={{0,4},{2,6},{4,0},{6,2},{8,12},{10,14},{12,8},{14,10},{16,20},{18,... | collective-permute-start | bytes 983048 | tf_op jit(solution)/shard_map/ppermute | solution.py:39
  56.0 8.0 %collective-permute-start.17 = (f32[16,3072]{1,0:T(8,128)}, f32[16,3072]{1,0:T(8,128)S(1)}, u32[]{:S(2)}, u32[]{:S(2)}) collective-permute-start(f32[16,3072]{1,0:T(8,128)} %get-tuple-element.44), channel_id=1, source_target_pairs={{0,2},{2,0},{4,6},{6,4},{8,10},{10,8},{12,14},{14,12},{16,18},{18,... | collective-permute-start | bytes 589832 | tf_op jit(solution)/shard_map/ppermute | solution.py:39
  56.8 12.9 %collective-permute-start.18 = (f32[16,3072]{1,0:T(8,128)}, f32[16,3072]{1,0:T(8,128)S(1)}, u32[]{:S(2)}, u32[]{:S(2)}) collective-permute-start(f32[16,3072]{1,0:T(8,128)} %get-tuple-element.45), channel_id=1, source_target_pairs={{0,4},{2,6},{4,0},{6,2},{8,12},{10,14},{12,8},{14,10},{16,20},{18,... | collective-permute-start | bytes 589832 | tf_op jit(solution)/shard_map/ppermute | solution.py:39
  58.3 11.4 %collective-permute-start.19 = (f32[16,3072]{1,0:T(8,128)}, f32[16,3072]{1,0:T(8,128)S(1)}, u32[]{:S(2)}, u32[]{:S(2)}) collective-permute-start(f32[16,3072]{1,0:T(8,128)} %get-tuple-element.46), channel_id=1, source_target_pairs={{0,6},{2,4},{4,2},{6,0},{8,14},{10,12},{12,10},{14,8},{16,22},{18,... | collective-permute-start | bytes 589832 | tf_op jit(solution)/shard_map/ppermute | solution.py:39
  59.6 31.9 %collective-permute-start.14 = (bf16[8,160,256]{2,1,0:T(8,128)(2,1)S(1)}, bf16[8,160,256]{2,1,0:T(8,128)(2,1)S(1)}, u32[]{:S(2)}, u32[]{:S(2)}) collective-permute-start(bf16[8,160,256]{2,1,0:T(8,128)(2,1)S(1)} %constant_dynamic-update-slice_fusion.refs_2_), channel_id=1, source_target_pairs={{0,4},{2,6},{4,0},{6,2},{8,12},{10,14},{12,8},{14,10},{16,20},{18,... | collective-permute-start | bytes 1966088 | tf_op jit(solution)/shard_map/ppermute | solution.py:39
  60.5 31.1 %collective-permute-start.15 = (bf16[8,160,256]{2,1,0:T(8,128)(2,1)S(1)}, bf16[8,160,256]{2,1,0:T(8,128)(2,1)S(1)}, u32[]{:S(2)}, u32[]{:S(2)}) collective-permute-start(bf16[8,160,256]{2,1,0:T(8,128)(2,1)S(1)} %constant_dynamic-update-slice_fusion.5.refs_3_), channel_id=1, source_target_pairs={{0,2},{2,0},{4,6},{6,4},{8,10},{10,8},{12,14},{14,12},{16,18},{18,... | collective-permute-start | bytes 1966088 | tf_op jit(solution)/shard_map/ppermute | solution.py:39
  73.6 7.4 %collective-permute-start.22 = (f32[16,768]{1,0:T(8,128)S(1)}, f32[16,768]{1,0:T(8,128)S(1)}, u32[]{:S(2)}, u32[]{:S(2)}) collective-permute-start(f32[16,768]{1,0:T(8,128)S(1)} %get-tuple-element.55), channel_id=1, source_target_pairs={{0,24},{2,26},{4,28},{6,30},{8,16},{10,18},{12,20},{14,22},{16,8},... | collective-permute-start | bytes 147464 | tf_op jit(solution)/shard_map/ppermute | solution.py:39
  82.1 16.5 %collective-permute-start.25 = (bf16[16,768]{1,0:T(8,128)(2,1)S(1)}, bf16[16,768]{1,0:T(8,128)(2,1)S(1)}, u32[]{:S(2)}, u32[]{:S(2)}) collective-permute-start(bf16[16,768]{1,0:T(8,128)(2,1)S(1)} %add_convert_fusion.1), channel_id=1, source_target_pairs={{0,8},{2,10},{4,12},{6,14},{8,0},{10,2},{12,4},{14,6},{16,24},{18,... | collective-permute-start | bytes 73736 | tf_op jit(solution)/shard_map/ppermute | solution.py:39
  82.2 16.4 %collective-permute-start.24 = (bf16[16,768]{1,0:T(8,128)(2,1)S(1)}, bf16[16,768]{1,0:T(8,128)(2,1)S(1)}, u32[]{:S(2)}, u32[]{:S(2)}) collective-permute-start(bf16[16,768]{1,0:T(8,128)(2,1)S(1)} %add_convert_fusion.1), channel_id=1, source_target_pairs={{0,16},{2,18},{4,20},{6,22},{8,24},{10,26},{12,28},{14,30},{16,0},... | collective-permute-start | bytes 73736 | tf_op jit(solution)/shard_map/ppermute | solution.py:39
  83.9 14.7 %collective-permute-start.23 = (bf16[16,768]{1,0:T(8,128)(2,1)S(1)}, bf16[16,768]{1,0:T(8,128)(2,1)S(1)}, u32[]{:S(2)}, u32[]{:S(2)}) collective-permute-start(bf16[16,768]{1,0:T(8,128)(2,1)S(1)} %add_convert_fusion.1), channel_id=1, source_target_pairs={{0,24},{2,26},{4,28},{6,30},{8,16},{10,18},{12,20},{14,22},{16,8},... | collective-permute-start | bytes 73736 | tf_op jit(solution)/shard_map/ppermute | solution.py:39
  99.3 16.7 %collective-permute-start.28 = (bf16[16,3072]{1,0:T(8,128)(2,1)}, bf16[16,3072]{1,0:T(8,128)(2,1)S(1)}, u32[]{:S(2)}, u32[]{:S(2)}) collective-permute-start(bf16[16,3072]{1,0:T(8,128)(2,1)} %shard_map.118), channel_id=1, source_target_pairs={{0,2},{2,0},{4,6},{6,4},{8,10},{10,8},{12,14},{14,12},{16,18},{18,... | collective-permute-start | bytes 294920 | tf_op jit(solution)/shard_map/ppermute | solution.py:39
  100.2 15.9 %collective-permute-start.27 = (bf16[16,3072]{1,0:T(8,128)(2,1)}, bf16[16,3072]{1,0:T(8,128)(2,1)S(1)}, u32[]{:S(2)}, u32[]{:S(2)}) collective-permute-start(bf16[16,3072]{1,0:T(8,128)(2,1)} %shard_map.118), channel_id=1, source_target_pairs={{0,4},{2,6},{4,0},{6,2},{8,12},{10,14},{12,8},{14,10},{16,20},{18,... | collective-permute-start | bytes 294920 | tf_op jit(solution)/shard_map/ppermute | solution.py:39
  101.3 14.7 %collective-permute-start.26 = (bf16[16,3072]{1,0:T(8,128)(2,1)}, bf16[16,3072]{1,0:T(8,128)(2,1)S(1)}, u32[]{:S(2)}, u32[]{:S(2)}) collective-permute-start(bf16[16,3072]{1,0:T(8,128)(2,1)} %shard_map.118), channel_id=1, source_target_pairs={{0,6},{2,4},{4,2},{6,0},{8,14},{10,12},{12,10},{14,8},{16,22},{18,... | collective-permute-start | bytes 294920 | tf_op jit(solution)/shard_map/ppermute | solution.py:39
  (20 other events, 139.3 us)
Sparse Core Ops, SparseCore 0:
  10.9 86.9 all-gather.2

commit v4 on v3

--- a/solution.py
+++ b/solution.py
@@ -260,16 +260,15 @@
     )(part, weight, gathered, mine, other, scaled_t, down_keep)
 
 
-def last_values_kernel(part_ref, weight_ref, normed_ref, low_ref, up_ref, first_ref, out_ref, total_ref):
+def last_values_kernel(part_ref, weight_ref, normed_ref, low_ref, up_ref, own_ref, theirs_ref, out_ref, total_ref):
     step = pl.program_id(0)
     blocks, _, rows, columns = weight_ref.shape
-    begin = first_ref.shape[1]
-    row_count = low_ref.shape[0]
+    begin = own_ref.shape[1]
 
     @pl.when(step == 0)
     def _():
-        out_ref[:, :begin] = first_ref[...]
-        total_ref[...] = 2.0 * dot(low_ref[...], up_ref[row_count:, begin:], 1, 0)
+        out_ref[:, :begin] = (own_ref[...] + theirs_ref[...]).astype(out_ref.dtype)
+        total_ref[...] = 2.0 * dot(low_ref[...], up_ref[:, begin:], 1, 0)
 
     total_ref[...] += dot(normed_ref[...], weight_ref[...].reshape(blocks * rows, columns), 1, 0)
 
@@ -278,7 +277,7 @@
         out_ref[:, begin:] = total_ref[...].astype(out_ref.dtype)
 
 
-def last_values(part, gathered, normed, low_rank, mine, first):
+def last_values(part, gathered, normed, low_rank, up_matrix, own, theirs):
     count, _, rows, columns = gathered.shape
     row_count = normed.shape[0]
     blocks = 4 * tile_blocks(rows, count // 2)
@@ -296,16 +295,17 @@
                 pl.BlockSpec((blocks, 1, rows, columns), lambda i, part: (i, part[0], 0, 0)),
                 pl.BlockSpec((row_count, width), lambda i, part: (0, i)),
                 whole(low_rank),
-                whole(mine),
-                whole(first),
+                whole(up_matrix),
+                whole(own),
+                whole(theirs),
             ],
-            out_specs=pl.BlockSpec((row_count, first.shape[1] + columns), lambda i, part: (0, 0)),
+            out_specs=pl.BlockSpec((row_count, own.shape[1] + columns), lambda i, part: (0, 0)),
             scratch_shapes=[pltpu.VMEM((row_count, columns), jnp.float32)],
         ),
-        out_shape=jax.ShapeDtypeStruct((row_count, first.shape[1] + columns), jnp.bfloat16),
+        out_shape=jax.ShapeDtypeStruct((row_count, own.shape[1] + columns), jnp.bfloat16),
         compiler_params=vmem_limit(56),
         cost_estimate=SHORT,
-    )(part, gathered, normed, low_rank, mine, first)
+    )(part, gathered, normed, low_rank, up_matrix, own, theirs)
 
 
 def prepare_kernel(
@@ -606,9 +606,8 @@
         got, plan = last_phase(held, masks, last)
 
     own, theirs, weight = forward(held + got, plan, normed, low_rank, mine, 0, cut)
-    values = (own + swap_cores(theirs)).astype(jnp.bfloat16)
     part = jnp.reshape(tensor_part, (1,))
-    values = last_values(part, gathered, normed, low_rank, mine, values)
+    values = last_values(part, gathered, normed, low_rank, mine[row_count:], own, swap_cores(theirs))
     gradient = input_gradient(part, weight, gathered, mine, other, scaled_t, down_keep)
     return (values, gradient, grad_a, grad_b)
 

time: 125 us -> 136 us (1.088)
  starting transfers between devices: 38.9 us -> 53.9 us
  waiting for transfers between devices: 26.3 us -> 21 us
  local copies, waits for them, and re-layouts: 5.11 us -> 7.38 us
    ppermute x3, starting transfers between devices: 1.29 us -> 10.6 us  [swap_cores(): return lax.ppermute(x, 'tensor', [(i, n - 1 - i) for i in range(n)])]
    ppermute x4, starting transfers between devices: 5.78 us -> 11.2 us  [first_phase(): slots.append(lax.ppermute(piece, ('dp', 'tensor'), pairs))]
    ppermute x22, waiting for transfers between devices: 25.4 us -> 21 us  [exchange(): lax.ppermute(x, 'dp', [(i, i ^ mask) for i in range(lax.axis_size('dp'))])]
    slice x0 -> x1, local copies, waits for them, and re-layouts: none -> 1.47 us  [shards(): mine[row_count:]]
  transfers between devices with their start and end apart: 30 -> 30, of which waited for: 11 -> 9; matrix products, arithmetic and copies ran while one was open for 3% -> 3% of each run, Pallas kernels for 27% -> 25%
where the time goes in v4:
time: 136 us
  starting transfers between devices  53.9 us (40%)
  Pallas kernels  34.2 us (25%)
  waiting for transfers between devices  21 us (15%)
  between operations  15.1 us (11%)
  local copies, waits for them, and re-layouts  7.38 us (5%)
  other arithmetic  4.36 us (3%)
    ppermute x22, starting transfers between devices, exchange(): lax.ppermute(x, 'dp', [(i, i ^ mask) for i in range(lax.axis_size('dp'))])  32.1 us
    ppermute x22, waiting for transfers between devices, exchange(): lax.ppermute(x, 'dp', [(i, i ^ mask) for i in range(lax.axis_size('dp'))])  21 us
    pallas_call x4, Pallas kernels, kernel_call(): pl.pallas_call(kernel, out_shape=tuple(outs), in_specs=[SMEM] * len(scala...  17.9 us
    ppermute x4, starting transfers between devices, first_phase(): slots.append(lax.ppermute(piece, ('dp', 'tensor'), pairs))  11.2 us
    ppermute x3, starting transfers between devices, swap_cores(): return lax.ppermute(x, 'tensor', [(i, n - 1 - i) for i in range(n)])  10.6 us
    pallas_call x1, Pallas kernels, input_gradient(): pl.pallas_call(gradient_kernel, grid_spec=pltpu.PrefetchScalarGridSpec(nu...  7.05 us
    pallas_call x1, Pallas kernels, last_values(): pl.pallas_call(last_values_kernel, grid_spec=pltpu.PrefetchScalarGridSpec...  5.43 us
    unnamed x32, local copies, waits for them, and re-layouts  4.1 us
  transfers between devices with their start and end apart: 30, of which 9 were waited for; matrix products, arithmetic and copies ran while one was open for 3% of the time, Pallas kernels for 25%

profile of v4, /device:TPU:0, one launch (start us, length us, event | category | flops | bytes accessed | tf_op | source)
XLA Modules:
  0.0 136.0 jit_solution(16649037037430319301)
XLA Ops:
  7.2 1.7 %fusion.2 = (bf16[320,256]{1,0:T(8,128)(2,1)S(1)}, bf16[320,256]{1,0:T(8,128)(2,1)}) fusion(bf16[320,512]{1,0:T(8,128)(2,1)} %param.10), kind=kLoop, calls=%fused_computation.40 | loop fusion | bytes 655360 | tf_op jit(solution)/shard_map/slice | solution.py:559
  8.9 3.8 %shard_map.111 = (bf16[576,512]{1,0:T(8,128)(2,1)}, s32[1]{0:T(128)}, bf16[4,80,128]{2,1,0:T(8,128)(2,1)}, bf16[4,80,128]{2,1,0:T(8,128)(2,1)}, bf16[4,80,128]{2...) custom-call(s32[8]{0:T(128)} %devices_ref.1, s32[8]{0:T(128)} %adapter_ref.1, s32[8]{0:T(128)} %valid_ref.1, ...), custom_call_target="tpu_custom_call" | custom-call | flops 1 | bytes 1 | tf_op jit(solution)/shard_map/pallas_call | solution.py:368
  12.8 3.0 %collective-permute-start = (bf16[4,80,128]{2,1,0:T(8,128)(2,1)}, bf16[4,80,128]{2,1,0:T(8,128)(2,1)S(1)}, u32[]{:S(2)}, u32[]{:S(2)}) collective-permute-start(bf16[4,80,128]{2,1,0:T(8,128)(2,1)} %get-tuple-element.28), channel_id=1, source_target_pairs={{0,2},{2,0},{4,6},{6,4},{8,10},{10,8},{12,14},{14,12},{16,18},{18,... | collective-permute-start | bytes 245768 | tf_op jit(solution)/shard_map/ppermute | solution.py:39
  18.8 2.5 %collective-permute-done.1.refs_2_ = bf16[4,80,128]{2,1,0:T(8,128)(2,1)S(1)} collective-permute-done((bf16[4,80,128]{2,1,0:T(8,128)(2,1)}, bf16[4,80,128]{2,1,0:T(8,128)(2,1)S(1)}, u32[]{:S(2)}, u32[]{:S(2)}) %collective-permute-start.1) | collective-permute-done | bytes 81952 | tf_op jit(solution)/shard_map/ppermute | solution.py:39
  23.5 1.8 %shard_map.112 = (bf16[4,80,128]{2,1,0:T(8,128)(2,1)}, bf16[4,80,128]{2,1,0:T(8,128)(2,1)}, bf16[4,80,128]{2,1,0:T(8,128)(2,1)}, bf16[4,80,128]{2,1,0:T(8,128)(2,1)}) custom-call(bf16[4,80,128]{2,1,0:T(8,128)(2,1)} %get-tuple-element.27.refs_0_, bf16[4,80,128]{2,1,0:T(8,128)(2,1)} %copy-done.11, bf16[4,80,128]{2,1,0:T(8,128)(2,1)} %copy-done.12, ...), custom_call_target="tpu_custom_call" | custom-call | flops 1 | bytes 1 | tf_op jit(solution)/shard_map/pallas_call | solution.py:93
  25.3 1.6 %collective-permute-start.3 = (bf16[4,80,128]{2,1,0:T(8,128)(2,1)}, bf16[4,80,128]{2,1,0:T(8,128)(2,1)S(1)}, u32[]{:S(2)}, u32[]{:S(2)}) collective-permute-start(bf16[4,80,128]{2,1,0:T(8,128)(2,1)} %get-tuple-element.32), channel_id=1, source_target_pairs={{0,8},{2,10},{4,12},{6,14},{8,0},{10,2},{12,4},{14,6},{16,24},{18,... | collective-permute-start | bytes 245768 | tf_op jit(solution)/shard_map/ppermute | solution.py:39
  26.9 2.6 %collective-permute-start.4 = (bf16[4,80,128]{2,1,0:T(8,128)(2,1)}, bf16[4,80,128]{2,1,0:T(8,128)(2,1)S(1)}, u32[]{:S(2)}, u32[]{:S(2)}) collective-permute-start(bf16[4,80,128]{2,1,0:T(8,128)(2,1)} %get-tuple-element.33), channel_id=1, source_target_pairs={{0,16},{2,18},{4,20},{6,22},{8,24},{10,26},{12,28},{14,30},{16,0},... | collective-permute-start | bytes 245768 | tf_op jit(solution)/shard_map/ppermute | solution.py:39
  31.3 5.7 %collective-permute-start.10 = (bf16[320,256]{1,0:T(8,128)(2,1)S(1)}, bf16[320,256]{1,0:T(8,128)(2,1)S(1)}, u32[]{:S(2)}, u32[]{:S(2)}) collective-permute-start(bf16[320,256]{1,0:T(8,128)(2,1)S(1)} %get-tuple-element.52), channel_id=1, source_target_pairs={{1,0},{3,2},{5,4},{7,6},{17,1},{19,3},{21,5},{23,7},{9,8},{11,10},... | collective-permute-start | bytes 491528 | tf_op jit(solution)/shard_map/ppermute | solution.py:132
  37.1 4.0 %collective-permute-start.11 = (bf16[320,256]{1,0:T(8,128)(2,1)S(1)}, bf16[320,256]{1,0:T(8,128)(2,1)S(1)}, u32[]{:S(2)}, u32[]{:S(2)}) collective-permute-start(bf16[320,256]{1,0:T(8,128)(2,1)S(1)} %get-tuple-element.52), channel_id=1, source_target_pairs={{9,0},{11,2},{13,4},{15,6},{25,1},{27,3},{29,5},{31,7},{1,8},{3,10... | collective-permute-start | bytes 491528 | tf_op jit(solution)/shard_map/ppermute | solution.py:132
  42.0 10.5 %collective-permute-start.6 = (bf16[4,4,80,128]{3,2,1,0:T(8,128)(2,1)S(1)}, bf16[4,4,80,128]{3,2,1,0:T(8,128)(2,1)S(1)}, u32[]{:S(2)}, u32[]{:S(2)}) collective-permute-start(bf16[4,4,80,128]{3,2,1,0:T(8,128)(2,1)S(1)} %pad_maximum_fusion.refs_1_), channel_id=1, source_target_pairs={{0,1},{1,0},{2,3},{3,2},{4,5},{5,4},{6,7},{7,6},{8,9},{9,8},{10,11... | collective-permute-start | bytes 983048 | tf_op jit(solution)/shard_map/ppermute | solution.py:35
  54.9 3.6 %shard_map.113 = (bf16[64,512]{1,0:T(8,128)(2,1)}, f32[64,2560]{1,0:T(8,128)}) custom-call(bf16[576,512]{1,0:T(8,128)(2,1)} %get-tuple-element.35.refs_0_.refs_3_.refs_1_.mine_ref, bf16[576,512]{1,0:T(8,128)(2,1)} %copy-done.1, bf16[512,5120]{1,0:T(8,128)(2,1)} %normed_ref.1), custom_call_target="tpu_custom_call" | custom-call | flops 1 | bytes 1 | tf_op jit(solution)/shard_map/pallas_call | solution.py:93
  59.2 6.8 %shard_map.114 = (bf16[512,64]{1,0:T(8,128)(2,1)}, bf16[2560,64]{1,0:T(8,128)(2,1)}, f32[64,512]{1,0:T(8,128)}, f32[16,3072]{1,0:T(8,128)}, f32[16,3072]{1,0:T(8...) custom-call(s32[1]{0:T(128)} %get-tuple-element.26.refs_0_, bf16[4,4,80,128]{3,2,1,0:T(8,128)(2,1)} %copy-done.2, ...), custom_call_target="tpu_custom_call" | custom-call | flops 1 | bytes 1 | tf_op jit(solution)/shard_map/pallas_call | solution.py:93
  67.0 2.0 %collective-permute-start.18 = (f32[16,3072]{1,0:T(8,128)}, f32[16,3072]{1,0:T(8,128)S(1)}, u32[]{:S(2)}, u32[]{:S(2)}) collective-permute-start(f32[16,3072]{1,0:T(8,128)} %get-tuple-element.45), channel_id=1, source_target_pairs={{0,4},{2,6},{4,0},{6,2},{8,12},{10,14},{12,8},{14,10},{16,20},{18,... | collective-permute-start | bytes 589832 | tf_op jit(solution)/shard_map/ppermute | solution.py:39
  70.7 2.1 %collective-permute-start.14 = (bf16[8,160,256]{2,1,0:T(8,128)(2,1)S(1)}, bf16[8,160,256]{2,1,0:T(8,128)(2,1)S(1)}, u32[]{:S(2)}, u32[]{:S(2)}) collective-permute-start(bf16[8,160,256]{2,1,0:T(8,128)(2,1)S(1)} %constant_dynamic-update-slice_fusion.refs_2_), channel_id=1, source_target_pairs={{0,4},{2,6},{4,0},{6,2},{8,12},{10,14},{12,8},{14,10},{16,20},{18,... | collective-permute-start | bytes 1966088 | tf_op jit(solution)/shard_map/ppermute | solution.py:39
  72.7 5.4 %collective-permute-done.17 = f32[16,3072]{1,0:T(8,128)S(1)} collective-permute-done((f32[16,3072]{1,0:T(8,128)}, f32[16,3072]{1,0:T(8,128)S(1)}, u32[]{:S(2)}, u32[]{:S(2)}) %collective-permute-start.17) | collective-permute-done | bytes 196640 | tf_op jit(solution)/shard_map/ppermute | solution.py:39
  78.4 5.2 %collective-permute-done.19 = f32[16,3072]{1,0:T(8,128)S(1)} collective-permute-done((f32[16,3072]{1,0:T(8,128)}, f32[16,3072]{1,0:T(8,128)S(1)}, u32[]{:S(2)}, u32[]{:S(2)}) %collective-permute-start.19) | collective-permute-done | bytes 196640 | tf_op jit(solution)/shard_map/ppermute | solution.py:39
  84.6 4.9 %collective-permute-start.20 = (f32[16,768]{1,0:T(8,128)S(1)}, f32[16,768]{1,0:T(8,128)S(1)}, u32[]{:S(2)}, u32[]{:S(2)}) collective-permute-start(f32[16,768]{1,0:T(8,128)S(1)} %get-tuple-element.54), channel_id=1, source_target_pairs={{0,8},{2,10},{4,12},{6,14},{8,0},{10,2},{12,4},{14,6},{16,24},{18,... | collective-permute-start | bytes 147464 | tf_op jit(solution)/shard_map/ppermute | solution.py:39
  90.4 1.6 %collective-permute-start.22 = (f32[16,768]{1,0:T(8,128)S(1)}, f32[16,768]{1,0:T(8,128)S(1)}, u32[]{:S(2)}, u32[]{:S(2)}) collective-permute-start(f32[16,768]{1,0:T(8,128)S(1)} %get-tuple-element.55), channel_id=1, source_target_pairs={{0,24},{2,26},{4,28},{6,30},{8,16},{10,18},{12,20},{14,22},{16,8},... | collective-permute-start | bytes 147464 | tf_op jit(solution)/shard_map/ppermute | solution.py:39
  92.0 3.4 %collective-permute-done.21 = f32[16,768]{1,0:T(8,128)S(1)} collective-permute-done((f32[16,768]{1,0:T(8,128)S(1)}, f32[16,768]{1,0:T(8,128)S(1)}, u32[]{:S(2)}, u32[]{:S(2)}) %collective-permute-start.21) | collective-permute-done | bytes 49184 | tf_op jit(solution)/shard_map/ppermute | solution.py:39
  96.4 1.6 %collective-permute-start.23 = (bf16[16,768]{1,0:T(8,128)(2,1)S(1)}, bf16[16,768]{1,0:T(8,128)(2,1)S(1)}, u32[]{:S(2)}, u32[]{:S(2)}) collective-permute-start(bf16[16,768]{1,0:T(8,128)(2,1)S(1)} %add_convert_fusion), channel_id=1, source_target_pairs={{0,24},{2,26},{4,28},{6,30},{8,16},{10,18},{12,20},{14,22},{16,8},... | collective-permute-start | bytes 73736 | tf_op jit(solution)/shard_map/ppermute | solution.py:39
  98.5 2.4 %collective-permute-start.25 = (bf16[16,768]{1,0:T(8,128)(2,1)S(1)}, bf16[16,768]{1,0:T(8,128)(2,1)S(1)}, u32[]{:S(2)}, u32[]{:S(2)}) collective-permute-start(bf16[16,768]{1,0:T(8,128)(2,1)S(1)} %add_convert_fusion), channel_id=1, source_target_pairs={{0,8},{2,10},{4,12},{6,14},{8,0},{10,2},{12,4},{14,6},{16,24},{18,... | collective-permute-start | bytes 73736 | tf_op jit(solution)/shard_map/ppermute | solution.py:39
  101.9 5.8 %shard_map.115 = (f32[512,256]{1,0:T(8,128)}, f32[512,256]{1,0:T(8,128)}, bf16[2,8,320,256]{3,2,1,0:T(8,128)(2,1)}) custom-call(bf16[512,64]{1,0:T(8,128)(2,1)} %get-tuple-element.37.refs_0_.low_ref, bf16[576,512]{1,0:T(8,128)(2,1)} %get-tuple-element.35.refs_0_.refs_3_.refs_1_.mine_ref, bf16[8,160,256]{2,1,0:T(8,128)(2,1)} %copy-done.5, ...), custom_call_target="tpu_custom_call" | custom-call | flops 1 | bytes 1 | tf_op jit(solution)/shard_map/pallas_call | solution.py:93
  114.1 7.0 %shard_map.117 = bf16[512,2560]{1,0:T(8,128)(2,1)} custom-call(s32[1]{0:T(128)} %bitcast.part_ref, bf16[2,8,320,256]{3,2,1,0:T(8,128)(2,1)} %get-tuple-element.40.weight_ref, bf16[16,2,320,256]{3,2,1,0:T(8,128)(2,1)} %bitcast.44, bf16[576,512]{1,0:T(8,128)(2,1)} %get-tuple-element.35.refs_0_.refs_3_.refs_1_.mine_ref, bf16[576,512]{1,0:T(8,128)(2,1)} %copy-done.1, ...), custom_call_target="tpu_custom_call" | custom-call | flops 1 | bytes 1 | tf_op jit(solution)/shard_map/pallas_call | solution.py:242
  122.0 5.4 %shard_map.116 = bf16[512,512]{1,0:T(8,128)(2,1)} custom-call(s32[1]{0:T(128)} %bitcast.part_ref, bf16[16,2,320,256]{3,2,1,0:T(8,128)(2,1)} %bitcast.45, bf16[512,5120]{1,0:T(8,128)(2,1)} %normed_ref.1, bf16[512,64]{1,0:T(8,128)(2,1)} %get-tuple-element.37.refs_0_.low_ref, bf16[64,512]{1,0:T(8,128)(2,1)} %slice.40.up_ref, ...), custom_call_target="tpu_custom_call" | custom-call | flops 1 | bytes 1 | tf_op jit(solution)/shard_map/pallas_call | solution.py:289
  (97 shorter events, 26.6 us)
Async XLA Ops:
  7.2 101.3 %all-gather.3.cloned.1.call-start = ((), (), s32[]{:S(2)}) async-start(), calls=%async_computation | async-start | bytes 5406720 | tf_op jit(solution)/shard_map/all_gather | solution.py:560
  26.9 10.1 %collective-permute-start.4 = (bf16[4,80,128]{2,1,0:T(8,128)(2,1)}, bf16[4,80,128]{2,1,0:T(8,128)(2,1)S(1)}, u32[]{:S(2)}, u32[]{:S(2)}) collective-permute-start(bf16[4,80,128]{2,1,0:T(8,128)(2,1)} %get-tuple-element.33), channel_id=1, source_target_pairs={{0,16},{2,18},{4,20},{6,22},{8,24},{10,26},{12,28},{14,30},{16,0},... | collective-permute-start | bytes 245768 | tf_op jit(solution)/shard_map/ppermute | solution.py:39
  29.5 11.6 %collective-permute-start.5 = (bf16[4,80,128]{2,1,0:T(8,128)(2,1)}, bf16[4,80,128]{2,1,0:T(8,128)(2,1)S(1)}, u32[]{:S(2)}, u32[]{:S(2)}) collective-permute-start(bf16[4,80,128]{2,1,0:T(8,128)(2,1)} %get-tuple-element.34), channel_id=1, source_target_pairs={{0,24},{2,26},{4,28},{6,30},{8,16},{10,18},{12,20},{14,22},{16,8},... | collective-permute-start | bytes 245768 | tf_op jit(solution)/shard_map/ppermute | solution.py:39
  29.8 12.3 %collective-permute-start.8 = (bf16[320,256]{1,0:T(8,128)(2,1)S(1)}, bf16[320,256]{1,0:T(8,128)(2,1)S(1)}, u32[]{:S(2)}, u32[]{:S(2)}) collective-permute-start(bf16[320,256]{1,0:T(8,128)(2,1)S(1)} %get-tuple-element.52), channel_id=1, source_target_pairs={{0,0},{2,2},{4,4},{6,6},{16,1},{18,3},{20,5},{22,7},{8,8},{10,10},... | collective-permute-start | bytes 491528 | tf_op jit(solution)/shard_map/ppermute | solution.py:132
  30.4 22.2 %collective-permute-start.9 = (bf16[320,256]{1,0:T(8,128)(2,1)S(1)}, bf16[320,256]{1,0:T(8,128)(2,1)S(1)}, u32[]{:S(2)}, u32[]{:S(2)}) collective-permute-start(bf16[320,256]{1,0:T(8,128)(2,1)S(1)} %get-tuple-element.52), channel_id=1, source_target_pairs={{8,0},{10,2},{12,4},{14,6},{24,1},{26,3},{28,5},{30,7},{0,8},{2,10... | collective-permute-start | bytes 491528 | tf_op jit(solution)/shard_map/ppermute | solution.py:132
  31.3 21.3 %collective-permute-start.10 = (bf16[320,256]{1,0:T(8,128)(2,1)S(1)}, bf16[320,256]{1,0:T(8,128)(2,1)S(1)}, u32[]{:S(2)}, u32[]{:S(2)}) collective-permute-start(bf16[320,256]{1,0:T(8,128)(2,1)S(1)} %get-tuple-element.52), channel_id=1, source_target_pairs={{1,0},{3,2},{5,4},{7,6},{17,1},{19,3},{21,5},{23,7},{9,8},{11,10},... | collective-permute-start | bytes 491528 | tf_op jit(solution)/shard_map/ppermute | solution.py:132
  37.1 15.6 %collective-permute-start.11 = (bf16[320,256]{1,0:T(8,128)(2,1)S(1)}, bf16[320,256]{1,0:T(8,128)(2,1)S(1)}, u32[]{:S(2)}, u32[]{:S(2)}) collective-permute-start(bf16[320,256]{1,0:T(8,128)(2,1)S(1)} %get-tuple-element.52), channel_id=1, source_target_pairs={{9,0},{11,2},{13,4},{15,6},{25,1},{27,3},{29,5},{31,7},{1,8},{3,10... | collective-permute-start | bytes 491528 | tf_op jit(solution)/shard_map/ppermute | solution.py:132
  41.1 13.0 %collective-permute-start.7 = (bf16[576,512]{1,0:T(8,128)(2,1)}, bf16[576,512]{1,0:T(8,128)(2,1)S(1)}, u32[]{:S(2)}, u32[]{:S(2)}) collective-permute-start(bf16[576,512]{1,0:T(8,128)(2,1)} %get-tuple-element.35.refs_0_.refs_3_.refs_1_.mine_ref), channel_id=1, source_target_pairs={{0,1},{1,0},{2,3},{3,2},{4,5},{5,4},{6,7},{7,6},{8,9},{9,8},{10,11... | collective-permute-start | bytes 1769480 | tf_op jit(solution)/shard_map/ppermute | solution.py:35
  42.0 16.4 %collective-permute-start.6 = (bf16[4,4,80,128]{3,2,1,0:T(8,128)(2,1)S(1)}, bf16[4,4,80,128]{3,2,1,0:T(8,128)(2,1)S(1)}, u32[]{:S(2)}, u32[]{:S(2)}) collective-permute-start(bf16[4,4,80,128]{3,2,1,0:T(8,128)(2,1)S(1)} %pad_maximum_fusion.refs_1_), channel_id=1, source_target_pairs={{0,1},{1,0},{2,3},{3,2},{4,5},{5,4},{6,7},{7,6},{8,9},{9,8},{10,11... | collective-permute-start | bytes 983048 | tf_op jit(solution)/shard_map/ppermute | solution.py:35
  52.7 16.8 %collective-permute-start.13 = (bf16[4,160,256]{2,1,0:T(8,128)(2,1)S(1)}, bf16[4,160,256]{2,1,0:T(8,128)(2,1)S(1)}, u32[]{:S(2)}, u32[]{:S(2)}) collective-permute-start(bf16[4,160,256]{2,1,0:T(8,128)(2,1)S(1)} %pad_maximum_fusion.2), channel_id=1, source_target_pairs={{0,4},{2,6},{4,0},{6,2},{8,12},{10,14},{12,8},{14,10},{16,20},{18,... | collective-permute-start | bytes 983048 | tf_op jit(solution)/shard_map/ppermute | solution.py:39
  52.9 17.8 %collective-permute-start.12 = (bf16[4,160,256]{2,1,0:T(8,128)(2,1)S(1)}, bf16[4,160,256]{2,1,0:T(8,128)(2,1)S(1)}, u32[]{:S(2)}, u32[]{:S(2)}) collective-permute-start(bf16[4,160,256]{2,1,0:T(8,128)(2,1)S(1)} %pad_maximum_fusion.1), channel_id=1, source_target_pairs={{0,2},{2,0},{4,6},{6,4},{8,10},{10,8},{12,14},{14,12},{16,18},{18,... | collective-permute-start | bytes 983048 | tf_op jit(solution)/shard_map/ppermute | solution.py:39
  66.0 12.1 %collective-permute-start.17 = (f32[16,3072]{1,0:T(8,128)}, f32[16,3072]{1,0:T(8,128)S(1)}, u32[]{:S(2)}, u32[]{:S(2)}) collective-permute-start(f32[16,3072]{1,0:T(8,128)} %get-tuple-element.44), channel_id=1, source_target_pairs={{0,2},{2,0},{4,6},{6,4},{8,10},{10,8},{12,14},{14,12},{16,18},{18,... | collective-permute-start | bytes 589832 | tf_op jit(solution)/shard_map/ppermute | solution.py:39
  67.0 11.4 %collective-permute-start.18 = (f32[16,3072]{1,0:T(8,128)}, f32[16,3072]{1,0:T(8,128)S(1)}, u32[]{:S(2)}, u32[]{:S(2)}) collective-permute-start(f32[16,3072]{1,0:T(8,128)} %get-tuple-element.45), channel_id=1, source_target_pairs={{0,4},{2,6},{4,0},{6,2},{8,12},{10,14},{12,8},{14,10},{16,20},{18,... | collective-permute-start | bytes 589832 | tf_op jit(solution)/shard_map/ppermute | solution.py:39
  69.0 14.6 %collective-permute-start.19 = (f32[16,3072]{1,0:T(8,128)}, f32[16,3072]{1,0:T(8,128)S(1)}, u32[]{:S(2)}, u32[]{:S(2)}) collective-permute-start(f32[16,3072]{1,0:T(8,128)} %get-tuple-element.46), channel_id=1, source_target_pairs={{0,6},{2,4},{4,2},{6,0},{8,14},{10,12},{12,10},{14,8},{16,22},{18,... | collective-permute-start | bytes 589832 | tf_op jit(solution)/shard_map/ppermute | solution.py:39
  69.6 31.3 %collective-permute-start.15 = (bf16[8,160,256]{2,1,0:T(8,128)(2,1)S(1)}, bf16[8,160,256]{2,1,0:T(8,128)(2,1)S(1)}, u32[]{:S(2)}, u32[]{:S(2)}) collective-permute-start(bf16[8,160,256]{2,1,0:T(8,128)(2,1)S(1)} %constant_dynamic-update-slice_fusion.5.refs_3_), channel_id=1, source_target_pairs={{0,2},{2,0},{4,6},{6,4},{8,10},{10,8},{12,14},{14,12},{16,18},{18,... | collective-permute-start | bytes 1966088 | tf_op jit(solution)/shard_map/ppermute | solution.py:39
  70.7 30.2 %collective-permute-start.14 = (bf16[8,160,256]{2,1,0:T(8,128)(2,1)S(1)}, bf16[8,160,256]{2,1,0:T(8,128)(2,1)S(1)}, u32[]{:S(2)}, u32[]{:S(2)}) collective-permute-start(bf16[8,160,256]{2,1,0:T(8,128)(2,1)S(1)} %constant_dynamic-update-slice_fusion.refs_2_), channel_id=1, source_target_pairs={{0,4},{2,6},{4,0},{6,2},{8,12},{10,14},{12,8},{14,10},{16,20},{18,... | collective-permute-start | bytes 1966088 | tf_op jit(solution)/shard_map/ppermute | solution.py:39
  84.6 7.4 %collective-permute-start.20 = (f32[16,768]{1,0:T(8,128)S(1)}, f32[16,768]{1,0:T(8,128)S(1)}, u32[]{:S(2)}, u32[]{:S(2)}) collective-permute-start(f32[16,768]{1,0:T(8,128)S(1)} %get-tuple-element.54), channel_id=1, source_target_pairs={{0,8},{2,10},{4,12},{6,14},{8,0},{10,2},{12,4},{14,6},{16,24},{18,... | collective-permute-start | bytes 147464 | tf_op jit(solution)/shard_map/ppermute | solution.py:39
  96.4 11.4 %collective-permute-start.23 = (bf16[16,768]{1,0:T(8,128)(2,1)S(1)}, bf16[16,768]{1,0:T(8,128)(2,1)S(1)}, u32[]{:S(2)}, u32[]{:S(2)}) collective-permute-start(bf16[16,768]{1,0:T(8,128)(2,1)S(1)} %add_convert_fusion), channel_id=1, source_target_pairs={{0,24},{2,26},{4,28},{6,30},{8,16},{10,18},{12,20},{14,22},{16,8},... | collective-permute-start | bytes 73736 | tf_op jit(solution)/shard_map/ppermute | solution.py:39
  98.0 9.8 %collective-permute-start.24 = (bf16[16,768]{1,0:T(8,128)(2,1)S(1)}, bf16[16,768]{1,0:T(8,128)(2,1)S(1)}, u32[]{:S(2)}, u32[]{:S(2)}) collective-permute-start(bf16[16,768]{1,0:T(8,128)(2,1)S(1)} %add_convert_fusion), channel_id=1, source_target_pairs={{0,16},{2,18},{4,20},{6,22},{8,24},{10,26},{12,28},{14,30},{16,0},... | collective-permute-start | bytes 73736 | tf_op jit(solution)/shard_map/ppermute | solution.py:39
  98.5 9.3 %collective-permute-start.25 = (bf16[16,768]{1,0:T(8,128)(2,1)S(1)}, bf16[16,768]{1,0:T(8,128)(2,1)S(1)}, u32[]{:S(2)}, u32[]{:S(2)}) collective-permute-start(bf16[16,768]{1,0:T(8,128)(2,1)S(1)} %add_convert_fusion), channel_id=1, source_target_pairs={{0,8},{2,10},{4,12},{6,14},{8,0},{10,2},{12,4},{14,6},{16,24},{18,... | collective-permute-start | bytes 73736 | tf_op jit(solution)/shard_map/ppermute | solution.py:39
  107.7 13.4 %collective-permute-start.16 = (f32[512,256]{1,0:T(8,128)}, f32[512,256]{1,0:T(8,128)S(1)}, u32[]{:S(2)}, u32[]{:S(2)}) collective-permute-start(f32[512,256]{1,0:T(8,128)} %get-tuple-element.39), channel_id=1, source_target_pairs={{0,1},{1,0},{2,3},{3,2},{4,5},{5,4},{6,7},{7,6},{8,9},{9,8},{10,11... | collective-permute-start | bytes 1572872 | tf_op jit(solution)/shard_map/ppermute | solution.py:35
  108.5 18.9 %collective-permute-start.26 = (bf16[16,3072]{1,0:T(8,128)(2,1)}, bf16[16,3072]{1,0:T(8,128)(2,1)S(1)}, u32[]{:S(2)}, u32[]{:S(2)}) collective-permute-start(bf16[16,3072]{1,0:T(8,128)(2,1)} %shard_map.118), channel_id=1, source_target_pairs={{0,6},{2,4},{4,2},{6,0},{8,14},{10,12},{12,10},{14,8},{16,22},{18,... | collective-permute-start | bytes 294920 | tf_op jit(solution)/shard_map/ppermute | solution.py:39
  109.5 17.9 %collective-permute-start.27 = (bf16[16,3072]{1,0:T(8,128)(2,1)}, bf16[16,3072]{1,0:T(8,128)(2,1)S(1)}, u32[]{:S(2)}, u32[]{:S(2)}) collective-permute-start(bf16[16,3072]{1,0:T(8,128)(2,1)} %shard_map.118), channel_id=1, source_target_pairs={{0,4},{2,6},{4,0},{6,2},{8,12},{10,14},{12,8},{14,10},{16,20},{18,... | collective-permute-start | bytes 294920 | tf_op jit(solution)/shard_map/ppermute | solution.py:39
  110.9 16.5 %collective-permute-start.28 = (bf16[16,3072]{1,0:T(8,128)(2,1)}, bf16[16,3072]{1,0:T(8,128)(2,1)S(1)}, u32[]{:S(2)}, u32[]{:S(2)}) collective-permute-start(bf16[16,3072]{1,0:T(8,128)(2,1)} %shard_map.118), channel_id=1, source_target_pairs={{0,2},{2,0},{4,6},{6,4},{8,10},{10,8},{12,14},{14,12},{16,18},{18,... | collective-permute-start | bytes 294920 | tf_op jit(solution)/shard_map/ppermute | solution.py:39
  (20 other events, 140.9 us)
Sparse Core Ops, SparseCore 0:
  10.9 77.7 all-gather.2
